TPU v7x, 32 devices: a whole 2x2x4 slice. The times are simulated.
32 devices in a mesh: wa: 4 (over y, x), ta: 8 (over z, core).
Axes of the slice: x: 2, y: 2, z: 4, core: 2. Of those that a mesh axis runs over, the one named last changes fastest.
Arguments:
- tokens: bfloat16 [768, 16384], P('wa', 'ta'), may hold values from -6 to 6
- seq_lengths: int32 [8], P('ta'), may hold values from 128 to 2048, as said below
- norm1_gain: float32 [768], P('wa'), may hold values from 0.5 to 1.5
- norm1_bias: float32 [768], P('wa'), may hold values from -4 to 4
- value_weight: bfloat16 [768, 768], P('ta', 'wa'), may hold values from -0.21875 to 0.21875
- value_bias: float32 [768], P('wa'), may hold values from -1.5 to 1.5
- synth_logits: bfloat16 [2048, 12, 2048], P('ta', 'wa'), may hold values from -8 to 8
- out_weight: bfloat16 [768, 768], P('wa', 'ta'), may hold values from -1.25 to 1.25
- out_bias: float32 [768], P('wa'), may hold values from -4 to 4
- norm2_gain: float32 [768], P('wa'), may hold values from 0.5 to 1.5
- norm2_bias: float32 [768], P('wa'), may hold values from -4 to 4
- up_weight: bfloat16 [768, 3072], P('wa', 'ta'), may hold values from -0.21875 to 0.21875
- up_bias: float32 [3072], P('wa'), may hold values from -4 to 4
- down_weight: bfloat16 [3072, 768], P('ta', 'wa'), may hold values from -0.109375 to 0.109375
- down_bias: float32 [768], P('wa'), may hold values from -4 to 4
- cotangent: bfloat16 [768, 16384], P('wa', 'ta'), may hold values from -6 to 6
Outputs:
- output: bfloat16 [768, 16384], P('wa', 'ta')
- tokens_grad: float32 [768, 16384], P('wa', 'ta')
- norm1_gain_grad: float32 [768], P('wa')
- norm1_bias_grad: float32 [768], P('wa')
- value_weight_grad: float32 [768, 768], P('ta', 'wa')
- value_bias_grad: float32 [768], P('wa')
- logits_grad: float32 [2048, 12, 2048], P('ta', 'wa')
- out_weight_grad: float32 [768, 768], P('wa', 'ta')
- out_bias_grad: float32 [768], P('wa')
- norm2_gain_grad: float32 [768], P('wa')
- norm2_bias_grad: float32 [768], P('wa')
- up_weight_grad: float32 [768, 3072], P('wa', 'ta')
- up_bias_grad: float32 [3072], P('wa')
- down_weight_grad: float32 [3072, 768], P('ta', 'wa')
- down_bias_grad: float32 [768], P('wa')
Inputs may be any that keep to these rules, and one draw needn't show every extreme that they name: `seq_lengths`: in every draw at least one packed row has the full length 2048.
All inputs are finite; a program needn't handle non-finite values.
Results may differ from a plain program's by a relative error of at most 0.007.
Values may be sent and summed in bfloat16 or wider, within the bound.
A program may use at most 256 MiB of HBM per device.

v0:
```python
import jax
import jax.numpy as jnp
from jax import lax
from jax.sharding import PartitionSpec as P

D = 768


EPSILON = 1e-05
NEGATIVE = -1e30
ALONG_FEATURES = (((1,), (1,)), ((), ()))
ALONG_ROWS = (((0,), (0,)), ((), ()))


def row_statistics(first_term, second_term):
    return lax.psum((jnp.sum(first_term, axis=1), jnp.sum(second_term, axis=1)), "wa")


def all_features(features_part):
    return lax.all_gather(features_part, "wa", axis=1, tiled=True)


def feature_share(partial_sum):
    return lax.psum_scatter(partial_sum, "wa", scatter_dimension=1, tiled=True)


def norm_forward(inputs, norm_gain, norm_bias):
    row_total, row_squares = row_statistics(inputs, inputs * inputs)
    row_mean = row_total / D
    variance = row_squares / D - row_mean * row_mean
    inverse = lax.rsqrt(variance + EPSILON)
    normed = (inputs - row_mean[:, None]) * inverse[:, None]
    return (normed * norm_gain + norm_bias, normed, inverse)


def norm_backward(incoming, normed, inverse, norm_gain):
    scaled = incoming * norm_gain
    row_total, row_along = row_statistics(scaled, scaled * normed)
    return inverse[:, None] * (scaled - row_total[:, None] / D - normed * row_along[:, None] / D)


def masked_scores(logit_rows, key_valid):
    return jnp.where(key_valid[:, None, None, :], logit_rows.astype(jnp.float32)[None], NEGATIVE)


def attend(logits_full, value_heads, key_valid, query_valid):
    seq_len = logits_full.shape[0]
    head_count = logits_full.shape[1]
    seq_count = value_heads.shape[0]
    block_rows = min(512, seq_len)
    blocks = seq_len // block_rows
    logit_blocks = logits_full.reshape(blocks, block_rows, head_count, seq_len)
    query_blocks = query_valid.reshape(seq_count, blocks, block_rows).transpose(1, 0, 2)

    def one_block(operands):
        logit_rows, query_rows = operands
        scores = masked_scores(logit_rows, key_valid)
        row_peak = jnp.max(scores, axis=-1, keepdims=True)
        exponent_terms = jnp.exp(scores - row_peak)
        row_sum = jnp.sum(exponent_terms, axis=-1, keepdims=True)
        probs_low = (exponent_terms / row_sum).astype(jnp.bfloat16)
        mixed_rows = jnp.einsum(
            "sqhk,skhd->sqhd", probs_low, value_heads, preferred_element_type=jnp.float32
        )
        return (mixed_rows * query_rows[:, :, None, None], row_peak, row_sum)

    mixed_rows, row_peak, row_sum = lax.map(one_block, (logit_blocks, query_blocks))
    return (mixed_rows.transpose(1, 0, 2, 3, 4), row_peak, row_sum)


def attend_back(logits_full, value_heads, key_valid, query_valid, grad_heads, row_peak, row_sum):
    seq_len = logits_full.shape[0]
    head_count = logits_full.shape[1]
    seq_count = value_heads.shape[0]
    head_dim = value_heads.shape[3]
    block_rows = min(512, seq_len)
    blocks = seq_len // block_rows
    logit_blocks = logits_full.reshape(blocks, block_rows, head_count, seq_len)
    query_blocks = query_valid.reshape(seq_count, blocks, block_rows).transpose(1, 0, 2)
    grad_blocks = grad_heads.reshape(seq_count, blocks, block_rows, head_count, head_dim).transpose(
        1, 0, 2, 3, 4
    )

    def one_block(carried, operands):
        logit_rows, grad_rows, query_rows, peak_rows, sum_rows = operands
        scores = masked_scores(logit_rows, key_valid)
        probabilities = jnp.exp(scores - peak_rows) / sum_rows
        grad_masked = grad_rows * query_rows[:, :, None, None].astype(jnp.bfloat16)
        dprobs = jnp.einsum(
            "sqhd,skhd->sqhk", grad_masked, value_heads, preferred_element_type=jnp.float32
        )
        carried = carried + jnp.einsum(
            "sqhk,sqhd->skhd",
            probabilities.astype(jnp.bfloat16),
            grad_masked,
            preferred_element_type=jnp.float32,
        )
        dscores = probabilities * (dprobs - jnp.sum(probabilities * dprobs, axis=-1, keepdims=True))
        return (carried, jnp.sum(dscores, axis=0))

    zero_values = jnp.zeros(value_heads.shape, jnp.float32)
    dvalue_heads, dlogit_blocks = lax.scan(
        one_block, zero_values, (logit_blocks, grad_blocks, query_blocks, row_peak, row_sum)
    )
    return (dvalue_heads, dlogit_blocks.reshape(seq_len, head_count, seq_len))


def on_device(
    tokens,
    seq_lengths,
    norm1_gain,
    norm1_bias,
    value_weight,
    value_bias,
    synth_logits,
    out_weight,
    out_bias,
    norm2_gain,
    norm2_bias,
    up_weight,
    up_bias,
    down_weight,
    down_bias,
    cotangent,
):
    rows_dev = tokens.shape[1]
    local_width = tokens.shape[0]
    seq_count = seq_lengths.shape[0]
    seq_len = synth_logits.shape[2]
    head_count = synth_logits.shape[1]
    head_dim = local_width // head_count
    value_cols, out_rows, up_rows, down_cols = (
        lax.all_gather(value_weight, "ta", axis=0, tiled=True),
        lax.all_gather(out_weight, "ta", axis=1, tiled=True),
        lax.all_gather(up_weight, "ta", axis=1, tiled=True),
        lax.all_gather(down_weight, "ta", axis=0, tiled=True),
    )
    up_block, down_block = (
        lax.all_to_all(up_rows.T, "wa", split_axis=0, concat_axis=1, tiled=True),
        lax.all_to_all(down_cols, "wa", split_axis=0, concat_axis=1, tiled=True),
    )
    inputs = tokens.T.astype(jnp.float32)
    pre_one, normed_one, inverse_one = norm_forward(inputs, norm1_gain, norm1_bias)
    layer_one = all_features(pre_one.astype(jnp.bfloat16))
    values = (
        jnp.dot(layer_one, value_cols, preferred_element_type=jnp.float32) + value_bias
    ).astype(jnp.bfloat16)
    value_heads = values.reshape(seq_count, seq_len, head_count, head_dim)
    positions = jnp.arange(seq_len)
    key_valid = positions[None, :] < seq_lengths[:, None]
    query_valid = key_valid.astype(jnp.float32)
    logits_full = lax.all_gather(synth_logits, "ta", axis=0, tiled=True)
    mixed_rows, row_peak, row_sum = attend(logits_full, value_heads, key_valid, query_valid)
    attended = mixed_rows.reshape(rows_dev, local_width).astype(jnp.bfloat16)
    branch = (
        feature_share(jnp.dot(attended, out_rows, preferred_element_type=jnp.float32)) + out_bias
    )
    resid = inputs + branch
    pre_two, normed_two, inverse_two = norm_forward(resid, norm2_gain, norm2_bias)
    layer_two = all_features(pre_two.astype(jnp.bfloat16))
    upper = (
        lax.dot_general(layer_two, up_block, ALONG_FEATURES, preferred_element_type=jnp.float32)
        + up_bias
    )
    hidden, gelu_back = jax.vjp(jax.nn.gelu, upper)
    hidden_low = hidden.astype(jnp.bfloat16)
    feed = (
        feature_share(jnp.dot(hidden_low, down_block, preferred_element_type=jnp.float32))
        + down_bias
    )
    output = (resid + feed).astype(jnp.bfloat16)
    cotangent_rows = cotangent.T
    grad_in = cotangent_rows.astype(jnp.float32)
    grad_full = all_features(cotangent_rows)
    dhidden = lax.dot_general(
        grad_full, down_block, ALONG_FEATURES, preferred_element_type=jnp.float32
    )
    dupper = gelu_back(dhidden)[0].astype(jnp.bfloat16)
    down_part = lax.dot_general(
        hidden_low, grad_full, ALONG_ROWS, preferred_element_type=jnp.float32
    )
    up_part = lax.dot_general(dupper, layer_two, ALONG_ROWS, preferred_element_type=jnp.float32)
    up_bias_part = jnp.sum(dupper.astype(jnp.float32), axis=0)
    down_bias_part = jnp.sum(grad_in, axis=0)
    dlayer_two = feature_share(jnp.dot(dupper, up_block, preferred_element_type=jnp.float32))
    gain_two_part = jnp.sum(dlayer_two * normed_two, axis=0)
    bias_two_part = jnp.sum(dlayer_two, axis=0)
    dresid = grad_in + norm_backward(dlayer_two, normed_two, inverse_two, norm2_gain)
    dbranch = dresid.astype(jnp.bfloat16)
    dbranch_full = all_features(dbranch)
    dattended = lax.dot_general(
        dbranch_full, out_rows, ALONG_FEATURES, preferred_element_type=jnp.float32
    ).astype(jnp.bfloat16)
    out_part = lax.dot_general(
        attended, dbranch_full, ALONG_ROWS, preferred_element_type=jnp.float32
    )
    out_bias_part = jnp.sum(dbranch.astype(jnp.float32), axis=0)
    grad_heads = dattended.reshape(seq_count, seq_len, head_count, head_dim)
    dvalue_heads, logits_part = attend_back(
        logits_full, value_heads, key_valid, query_valid, grad_heads, row_peak, row_sum
    )
    dvalues = dvalue_heads.reshape(rows_dev, local_width).astype(jnp.bfloat16)
    value_part = lax.dot_general(layer_one, dvalues, ALONG_ROWS, preferred_element_type=jnp.float32)
    value_bias_part = jnp.sum(dvalues.astype(jnp.float32), axis=0)
    dlayer_one = feature_share(
        lax.dot_general(dvalues, value_cols, ALONG_FEATURES, preferred_element_type=jnp.float32)
    )
    gain_one_part = jnp.sum(dlayer_one * normed_one, axis=0)
    bias_one_part = jnp.sum(dlayer_one, axis=0)
    tokens_grad = dresid + norm_backward(dlayer_one, normed_one, inverse_one, norm1_gain)
    up_back, down_back = (
        lax.all_to_all(up_part, "wa", split_axis=1, concat_axis=0, tiled=True),
        lax.all_to_all(down_part, "wa", split_axis=1, concat_axis=0, tiled=True),
    )
    value_grad, out_grad, up_grad, down_grad, logits_grad = (
        lax.psum_scatter(value_part, "ta", scatter_dimension=0, tiled=True),
        lax.psum_scatter(out_part, "ta", scatter_dimension=1, tiled=True),
        lax.psum_scatter(up_back, "ta", scatter_dimension=0, tiled=True),
        lax.psum_scatter(down_back, "ta", scatter_dimension=0, tiled=True),
        lax.psum_scatter(logits_part, "ta", scatter_dimension=0, tiled=True),
    )
    vector_grads = lax.psum(
        (
            gain_one_part,
            bias_one_part,
            value_bias_part,
            out_bias_part,
            gain_two_part,
            bias_two_part,
            up_bias_part,
            down_bias_part,
        ),
        "ta",
    )
    return (
        output.T,
        tokens_grad.T,
        vector_grads[0],
        vector_grads[1],
        value_grad,
        vector_grads[2],
        logits_grad,
        out_grad,
        vector_grads[3],
        vector_grads[4],
        vector_grads[5],
        up_grad.T,
        vector_grads[6],
        down_grad,
        vector_grads[7],
    )


def solution(mesh):
    placed = (
        P("wa", "ta"),
        P("ta"),
        P("wa"),
        P("wa"),
        P("ta", "wa"),
        P("wa"),
        P("ta", "wa", None),
        P("wa", "ta"),
        P("wa"),
        P("wa"),
        P("wa"),
        P("wa", "ta"),
        P("wa"),
        P("ta", "wa"),
        P("wa"),
        P("wa", "ta"),
    )
    return jax.shard_map(
        on_device,
        mesh=mesh,
        in_specs=placed,
        out_specs=(
            P("wa", "ta"),
            P("wa", "ta"),
            P("wa"),
            P("wa"),
            P("ta", "wa"),
            P("wa"),
            P("ta", "wa", None),
            P("wa", "ta"),
            P("wa"),
            P("wa"),
            P("wa"),
            P("wa", "ta"),
            P("wa"),
            P("ta", "wa"),
            P("wa"),
        ),
        check_vma=False,
    )
```

profile of v0, /device:TPU:0, one launch (start us, length us, event | category | flops | bytes accessed | tf_op | source)
XLA Modules:
  0.0 1698.0 jit_solution(14957910379818049333)
XLA Ops:
  9.8 17.6 %all-reduce.4 = (f32[2048]{0:T(1024)S(1)}, f32[2048]{0:T(1024)S(1)}) all-reduce(f32[2048]{0:T(1024)S(1)} %fusion.68, f32[2048]{0:T(1024)S(1)} %convert_reduce_fusion.3), channel_id=1, replica_groups=mesh['wa'=4,'ta'=8] {'wa'}, use_global_device_ids=true, to_apply=%region_3.0 | all-reduce | flops 4096 | bytes 32768 | tf_op jit(solution)/shard_map/psum | solution.py:16
  32.7 14.9 all_gather.30
  47.6 14.4 all_gather.29
  62.0 12.0 all-gather.10.cloned.1.call-done
  76.7 218.8 %all-gather.8.cloned.1.call-done = bf16[2048,3,2048]{2,0,1:T(8,128)(2,1)} async-done(((bf16[256,3,2048]{2,0,1:T(8,128)(2,1)}), bf16[2048,3,2048]{2,0,1:T(8,128)(2,1)}) %all-gather.8.cloned.1.call-update) | async-done | bytes 25165840 | tf_op jit(solution)/shard_map/all_gather | solution.py:152
  295.5 21.0 %copy.51 = bf16[4,512,3,2048]{3,1,2,0:T(8,128)(2,1)} copy(bf16[4,512,3,2048]{3,1,0,2:T(8,128)(2,1)} %bitcast.224) | data formatting | bytes 50331648
  316.5 62.8 %while.28 = (s32[]{:T(128)}, bf16[4,1,512,3,64]{2,4,3,1,0:T(8,128)(2,1)S(1)}, f32[4,1,512,3,1]{2,3,4,1,0:T(4,128)}, f32[4,1,512,3,1]{2,3,4,1,0:T(4,128)}, bf16[4...) while((s32[]{:T(128)}, ...), condition=%wide.region_7.8_spmd.clone, body=%wide.region_4.7_spmd.clone.sunk | while | flops 440499200 | bytes 20132984 | solution.py:67
  385.9 67.3 %reduce-scatter.12.cloned.1.call-done = f32[2048,192]{0,1:T(8,128)} async-done(((f32[2048,768]{0,1:T(8,128)}), f32[2048,192]{0,1:T(8,128)}) %reduce-scatter.12.cloned.1.call-update) | async-done | bytes 1572880 | tf_op jit(solution)/shard_map/reduce_scatter | solution.py:24
  455.1 15.1 all-reduce.3
  483.7 18.3 %all-gather.16.cloned.1.call-done = bf16[3072,192]{0,1:T(8,128)(2,1)} async-done(((bf16[384,192]{0,1:T(8,128)(2,1)}), bf16[3072,192]{0,1:T(8,128)(2,1)}) %all-gather.16.cloned.1.call-update) | async-done | bytes 1179664 | tf_op jit(solution)/shard_map/all_gather | solution.py:136
  509.2 47.6 %all-gather.12.cloned.1.call-done = bf16[2048,768]{0,1:T(8,128)(2,1)} async-done(((bf16[2048,192]{0,1:T(8,128)(2,1)}), bf16[2048,768]{0,1:T(8,128)(2,1)}) %all-gather.12.cloned.1.call-update) | async-done | bytes 3145744 | tf_op jit(solution)/shard_map/all_gather | solution.py:20
  564.4 38.2 %all-gather.18.cloned.1.call-done = bf16[2048,768]{0,1:T(8,128)(2,1)} async-done(((bf16[2048,192]{0,1:T(8,128)(2,1)}), bf16[2048,768]{0,1:T(8,128)(2,1)}) %all-gather.18.cloned.1.call-update) | async-done | bytes 3145744 | tf_op jit(solution)/shard_map/all_gather | solution.py:20
  602.6 12.5 convert_reduce_fusion.1
  621.4 70.3 %reduce-scatter.16.cloned.1.call-done = f32[2048,192]{0,1:T(8,128)} async-done(((f32[2048,768]{0,1:T(8,128)}), f32[2048,192]{0,1:T(8,128)}) %reduce-scatter.16.cloned.1.call-update) | async-done | bytes 1572880 | tf_op jit(solution)/shard_map/reduce_scatter | solution.py:24
  694.5 16.3 all-reduce.2
  715.2 43.7 %all-gather.20.cloned.1.call-done = bf16[2048,768]{0,1:T(8,128)(2,1)} async-done(((bf16[2048,192]{0,1:T(8,128)(2,1)}), bf16[2048,768]{0,1:T(8,128)(2,1)}) %all-gather.20.cloned.1.call-update) | async-done | bytes 3145744 | tf_op jit(solution)/shard_map/all_gather | solution.py:20
  769.6 127.9 %while.29 = (s32[]{:T(128)}, f32[1,2048,3,64]{1,3,2,0:T(8,128)S(1)}, f32[4,512,3,2048]{3,1,0,2:T(8,128)}, bf16[4,1,512,3,64]{2,4,3,1,0:T(8,128)(2,1)}, bf16[4,1,...) while((s32[]{:T(128)}, ...), condition=%wide.region_21.22_spmd.clone, body=%wide.region_19.21_spmd.clone.sunk | while | flops 859767296 | bytes 164846288 | solution.py:102
  782.1 8.0 fusion.123
  790.1 11.8 bitcast_dynamic-update-slice_fusion.6
  822.2 11.6 bitcast_dynamic-update-slice_fusion.6
  846.1 8.0 fusion.123
  854.1 11.6 bitcast_dynamic-update-slice_fusion.6
  878.0 8.0 fusion.123
  886.0 11.6 bitcast_dynamic-update-slice_fusion.6
  915.0 54.6 %all_to_all.76 = f32[768,4,192]{0,2,1:T(8,128)S(1)} all-to-all(f32[768,4,192]{0,2,1:T(8,128)S(1)} %bitcast.235), channel_id=1, replica_groups=mesh['wa'=4,'ta'=8] {'wa'}, dimensions={1} | all-to-all | bytes 4718592 | tf_op jit(solution)/shard_map/all_to_all | solution.py:213
  976.8 43.8 %all_to_all.77 = f32[768,4,192]{0,2,1:T(8,128)S(1)} all-to-all(f32[768,4,192]{0,2,1:T(8,128)S(1)} %bitcast.236), channel_id=1, replica_groups=mesh['wa'=4,'ta'=8] {'wa'}, dimensions={1} | all-to-all | bytes 4718592 | tf_op jit(solution)/shard_map/all_to_all | solution.py:212
  1030.8 15.0 all-reduce.1
  1045.8 49.4 %reduce-scatter.14.cloned.1.call-done = f32[2048,192]{0,1:T(8,128)} async-done(((f32[2048,768]{0,1:T(8,128)}), f32[2048,192]{0,1:T(8,128)}) %reduce-scatter.14.cloned.1.call-update) | async-done | bytes 1572880 | tf_op jit(solution)/shard_map/reduce_scatter | solution.py:24
  1100.6 28.9 %all-reduce = (f32[192]{0:T(256)}, f32[192]{0:T(256)}, f32[192]{0:T(256)}, f32[192]{0:T(256)}, f32[192]{0:T(256)}, /*index=5*/f32[192]{0:T(256)}, f32[768]{0:T(1024)}, f32[192]{0:T(256)}) all-reduce(f32[192]{0:T(256)S(1)} %get-tuple-element.238, f32[192]{0:T(256)S(1)} %get-tuple-element.243, ...), channel_id=1, replica_groups=mesh['wa'=4,'ta'=8] {'ta'}, use_global_device_ids=true, to_apply=%region_28.29 | all-reduce | flops 2112 | bytes 16896 | tf_op jit(solution)/shard_map/psum | solution.py:222
  1134.6 38.5 %reduce-scatter.24.cloned.1.call-done = f32[384,192]{0,1:T(8,128)} async-done(((f32[3072,192]{0,1:T(8,128)}), f32[384,192]{0,1:T(8,128)}) %reduce-scatter.24.cloned.1.call-update) | async-done | bytes 294928 | tf_op jit(solution)/shard_map/reduce_scatter | solution.py:218
  1173.1 33.7 %reduce-scatter.20.cloned.1.call-done = f32[96,192]{1,0:T(8,128)} async-done(((f32[768,192]{1,0:T(8,128)}), f32[96,192]{1,0:T(8,128)}) %reduce-scatter.20.cloned.1.call-update) | async-done | bytes 73744 | tf_op jit(solution)/shard_map/reduce_scatter | solution.py:216
  1206.8 484.2 %reduce-scatter.22.cloned.1.call-done = f32[256,3,2048]{2,0,1:T(8,128)} async-done(((f32[2048,3,2048]{2,0,1:T(8,128)}), f32[256,3,2048]{2,0,1:T(8,128)}) %reduce-scatter.22.cloned.1.call-update) | async-done | bytes 6291472 | tf_op jit(solution)/shard_map/reduce_scatter | solution.py:220
  (221 shorter events, 235.7 us)
Async XLA Ops:
  7.2 66.8 %all-gather.10.cloned.1.call-start = ((), (), s32[]{:S(2)}) async-start(), calls=%async_computation.14 | async-start | bytes 3932160 | tf_op jit(solution)/shard_map/all_gather | solution.py:20
  30.5 265.0 %all-gather.8.cloned.1.call-start = ((), (), s32[]{:S(2)}) async-start(), calls=%async_computation.13 | async-start | bytes 28311552 | tf_op jit(solution)/shard_map/all_gather | solution.py:152
  31.2 422.0 %reduce-scatter.12.cloned.1.call-start = ((), (), s32[]{:S(2)}) async-start(), calls=%async_computation.15 | async-start | bytes 7864320 | tf_op jit(solution)/shard_map/reduce_scatter | solution.py:24
  384.7 68.6 %copy-start.3 = (bf16[192,2048]{1,0:T(8,128)(2,1)S(1)}, bf16[192,2048]{1,0:T(8,128)(2,1)}, u32[]{:S(2)}) copy-start(bf16[192,2048]{1,0:T(8,128)(2,1)} %param.20) | copy-start | bytes 2359300
  384.7 68.6 %copy-start.35 = (f32[192]{0:T(256)S(1)}, f32[192]{0:T(256)}, u32[]{:S(2)}) copy-start(f32[192]{0:T(256)} %param.28) | copy-start | bytes 2308
  384.7 85.5 %copy-start.28 = (f32[192]{0:T(256)S(1)}, f32[192]{0:T(256)}, u32[]{:S(2)}) copy-start(f32[192]{0:T(256)} %param.29) | copy-start | bytes 2308
  384.7 85.5 %copy-start.36 = (f32[192]{0:T(256)S(1)}, f32[192]{0:T(256)}, u32[]{:S(2)}) copy-start(f32[192]{0:T(256)} %param.30) | copy-start | bytes 2308
  384.7 93.0 %all-gather.14.cloned.1.call-start = ((), (), s32[]{:S(2)}) async-start(), calls=%async_computation.17 | async-start | bytes 1327104 | tf_op jit(solution)/shard_map/all_gather | solution.py:135
  385.3 116.7 %all-gather.16.cloned.1.call-start = ((), (), s32[]{:S(2)}) async-start(), calls=%async_computation.18 | async-start | bytes 1327104 | tf_op jit(solution)/shard_map/all_gather | solution.py:136
  385.9 170.9 %all-gather.12.cloned.1.call-start = ((), (), s32[]{:S(2)}) async-start(), calls=%async_computation.16 | async-start | bytes 3932160 | tf_op jit(solution)/shard_map/all_gather | solution.py:20
  455.1 256.5 %copy-start.1 = (f32[2048,192]{0,1:T(8,128)}, f32[2048,192]{0,1:T(8,128)S(1)}, u32[]{:S(2)}) copy-start(f32[2048,192]{0,1:T(8,128)S(1)} %get-tuple-element.306) | copy-start | bytes 4718596
  470.2 241.4 %copy-start.15 = (f32[2048]{0:T(1024)}, f32[2048]{0:T(1024)S(1)}, u32[]{:S(2)}) copy-start(f32[2048]{0:T(1024)S(1)} %get-tuple-element.317) | copy-start | bytes 24580
  470.2 241.4 %copy-start.17 = (f32[2048]{0:T(1024)}, f32[2048]{0:T(1024)S(1)}, u32[]{:S(2)}) copy-start(f32[2048]{0:T(1024)S(1)} %get-tuple-element.318) | copy-start | bytes 24580
  471.5 131.1 %all-gather.18.cloned.1.call-start = ((), (), s32[]{:S(2)}) async-start(), calls=%async_computation.20 | async-start | bytes 3932160 | tf_op jit(solution)/shard_map/all_gather | solution.py:20
  480.1 24.3 %all-to-all-start = ((bf16[4,768,192]{1,2,0:T(8,128)(2,1)}), bf16[4,768,192]{1,2,0:T(8,128)(2,1)S(1)}, u32[]{:S(2)}, u32[]{:S(2)}) async-start(bf16[4,768,192]{1,2,0:T(8,128)(2,1)} %bitcast.191), calls=%async_computation.1 | async-start | bytes 2359296 | tf_op jit(solution)/shard_map/all_to_all | solution.py:139
  505.5 58.9 %all-to-all-start.1 = ((bf16[4,768,192]{1,2,0:T(8,128)(2,1)}), bf16[4,768,192]{1,2,0:T(8,128)(2,1)S(1)}, u32[]{:S(2)}, u32[]{:S(2)}) async-start(bf16[4,768,192]{1,2,0:T(8,128)(2,1)} %bitcast.190), calls=%async_computation.2 | async-start | bytes 2359296 | tf_op jit(solution)/shard_map/all_to_all | solution.py:140
  509.0 182.7 %reduce-scatter.16.cloned.1.call-start = ((), (), s32[]{:S(2)}) async-start(), calls=%async_computation.21 | async-start | bytes 7864320 | tf_op jit(solution)/shard_map/reduce_scatter | solution.py:24
  621.3 137.5 %all-gather.20.cloned.1.call-start = ((), (), s32[]{:S(2)}) async-start(), calls=%async_computation.22 | async-start | bytes 3932160 | tf_op jit(solution)/shard_map/all_gather | solution.py:20
  714.9 312.0 %reduce-scatter.28.cloned.1.call-start = ((), (), s32[]{:S(2)}) async-start(), calls=%async_computation.28 | async-start | bytes 884736
  769.6 259.1 %reduce-scatter.18.cloned.1.call-start = ((), (), s32[]{:S(2)}) async-start(), calls=%async_computation.23 | async-start | bytes 7864320 | tf_op jit(solution)/shard_map/reduce_scatter | solution.py:24
  769.6 128.1 %copy-start.10 = (bf16[768,192]{1,0:T(8,128)(2,1)S(1)}, bf16[768,192]{1,0:T(8,128)(2,1)}, u32[]{:S(2)}) copy-start(bf16[768,192]{1,0:T(8,128)(2,1)} %copy-done.9) | copy-start | bytes 884740
  901.3 193.9 %reduce-scatter.14.cloned.1.call-start = ((), (), s32[]{:S(2)}) async-start(), calls=%async_computation.19 | async-start | bytes 7864320 | tf_op jit(solution)/shard_map/reduce_scatter | solution.py:24
  909.3 225.3 %reduce-scatter.26.cloned.1.call-start = ((), (), s32[]{:S(2)}) async-start(), calls=%async_computation.27 | async-start | bytes 2654208 | tf_op jit(solution)/shard_map/reduce_scatter | solution.py:219
  971.3 201.8 %reduce-scatter.24.cloned.1.call-start = ((), (), s32[]{:S(2)}) async-start(), calls=%async_computation.26 | async-start | bytes 2654208 | tf_op jit(solution)/shard_map/reduce_scatter | solution.py:218
  1022.3 184.5 %reduce-scatter.20.cloned.1.call-start = ((), (), s32[]{:S(2)}) async-start(), calls=%async_computation.24 | async-start | bytes 884736 | tf_op jit(solution)/shard_map/reduce_scatter | solution.py:216
  1026.2 664.8 %reduce-scatter.22.cloned.1.call-start = ((), (), s32[]{:S(2)}) async-start(), calls=%async_computation.25 | async-start | bytes 56623104 | tf_op jit(solution)/shard_map/reduce_scatter | solution.py:220
  1026.3 68.9 %copy-start.16 = (f32[2048]{0:T(1024)S(1)}, f32[2048]{0:T(1024)}, u32[]{:S(2)}) copy-start(f32[2048]{0:T(1024)} %copy-done.15) | copy-start | bytes 24580
  1026.3 68.9 %copy-start.18 = (f32[2048]{0:T(1024)S(1)}, f32[2048]{0:T(1024)}, u32[]{:S(2)}) copy-start(f32[2048]{0:T(1024)} %copy-done.17) | copy-start | bytes 24580
  1026.3 68.8 %copy-start.24 = (f32[2048]{0:T(1024)S(1)}, f32[2048]{0:T(1024)}, u32[]{:S(2)}) copy-start(f32[2048]{0:T(1024)} %copy-done.23) | copy-start | bytes 24580
  1026.3 68.8 %copy-start.27 = (f32[2048]{0:T(1024)S(1)}, f32[2048]{0:T(1024)}, u32[]{:S(2)}) copy-start(f32[2048]{0:T(1024)} %get-tuple-element.292) | copy-start | bytes 24580
  1026.4 68.8 %copy-start.29 = (f32[192]{0:T(256)S(1)}, f32[192]{0:T(256)}, u32[]{:S(2)}) copy-start(f32[192]{0:T(256)} %param.29) | copy-start | bytes 2308
  1026.4 68.8 %copy-start.37 = (f32[192]{0:T(256)S(1)}, f32[192]{0:T(256)}, u32[]{:S(2)}) copy-start(f32[192]{0:T(256)} %param.34) | copy-start | bytes 2308
  (35 other events, 566.9 us)
Sparse Core Ops, SparseCore 0:
  30.6 43.3 all-gather.9
  75.6 219.8 all-gather.7
  384.8 68.3 reduce-scatter.11
  454.7 22.9 all-gather.13
  479.2 22.7 all-gather.15
  504.2 52.5 all-gather.11
  558.6 43.9 all-gather.17
  621.5 70.2 reduce-scatter.15
  715.0 43.7 all-gather.19
  769.7 31.5 reduce-scatter.27
  901.4 119.9 reduce-scatter.17
  1024.5 70.5 reduce-scatter.13
  1098.2 36.3 reduce-scatter.25
  1137.4 35.6 reduce-scatter.23
  1175.9 30.8 reduce-scatter.19
  1209.6 481.3 reduce-scatter.21
where the time goes:
time: 1710 us; the launch traced here: 1700 us
  waiting for transfers between devices  1140 us (67%)
  blocking collectives  221 us (13%)
  matrix products  142 us (8%)
  other arithmetic  112 us (7%)
  local copies, waits for them, and re-layouts  64.5 us (4%)
    reduce_scatter x1, waiting for transfers between devices, on_device(): lax.psum_scatter(logits_part, 'ta', scatter_dimension=0, tiled=True)  484 us
    all_gather x1, waiting for transfers between devices, on_device(): logits_full = lax.all_gather(synth_logits, 'ta', axis=0, tiled=True)  219 us
    reduce_scatter x4, waiting for transfers between devices, feature_share(): return lax.psum_scatter(partial_sum, 'wa', scatter_dimension=1, tiled=True)  187 us
    all_gather x4, waiting for transfers between devices, all_features(): return lax.all_gather(features_part, 'wa', axis=1, tiled=True)  141 us
    psum x4, blocking collectives, row_statistics(): lax.psum((jnp.sum(first_term, axis=1), jnp.sum(second_term, axis=1)), 'wa')  64.1 us
    all_to_all x1, blocking collectives, on_device(): lax.all_to_all(down_part, 'wa', split_axis=1, concat_axis=0, tiled=True)  54.6 us
    dynamic_update_slice x4, other arithmetic, attend_back(): lax.scan(one_block, zero_values, (logit_blocks, grad_blocks, query_blocks...  46.6 us
    all_to_all x1, blocking collectives, on_device(): lax.all_to_all(up_part, 'wa', split_axis=1, concat_axis=0, tiled=True)  43.8 us
  transfers between devices with their start and end apart: 18, of which 14 were waited for; matrix products, arithmetic and copies ran while one was open for 10% of the time, Pallas kernels for 0%

commit v1 on v0

--- a/solution.py
+++ b/solution.py
@@ -7,7 +7,6 @@
 
 
 EPSILON = 1e-05
-NEGATIVE = -1e30
 ALONG_FEATURES = (((1,), (1,)), ((), ()))
 ALONG_ROWS = (((0,), (0,)), ((), ()))
 
@@ -39,70 +38,32 @@
     return inverse[:, None] * (scaled - row_total[:, None] / D - normed * row_along[:, None] / D)
 
 
-def masked_scores(logit_rows, key_valid):
-    return jnp.where(key_valid[:, None, None, :], logit_rows.astype(jnp.float32)[None], NEGATIVE)
-
-
-def attend(logits_full, value_heads, key_valid, query_valid):
-    seq_len = logits_full.shape[0]
-    head_count = logits_full.shape[1]
-    seq_count = value_heads.shape[0]
-    block_rows = min(512, seq_len)
-    blocks = seq_len // block_rows
-    logit_blocks = logits_full.reshape(blocks, block_rows, head_count, seq_len)
-    query_blocks = query_valid.reshape(seq_count, blocks, block_rows).transpose(1, 0, 2)
-
-    def one_block(operands):
-        logit_rows, query_rows = operands
-        scores = masked_scores(logit_rows, key_valid)
-        row_peak = jnp.max(scores, axis=-1, keepdims=True)
-        exponent_terms = jnp.exp(scores - row_peak)
-        row_sum = jnp.sum(exponent_terms, axis=-1, keepdims=True)
-        probs_low = (exponent_terms / row_sum).astype(jnp.bfloat16)
-        mixed_rows = jnp.einsum(
-            "sqhk,skhd->sqhd", probs_low, value_heads, preferred_element_type=jnp.float32
-        )
-        return (mixed_rows * query_rows[:, :, None, None], row_peak, row_sum)
-
-    mixed_rows, row_peak, row_sum = lax.map(one_block, (logit_blocks, query_blocks))
-    return (mixed_rows.transpose(1, 0, 2, 3, 4), row_peak, row_sum)
-
-
-def attend_back(logits_full, value_heads, key_valid, query_valid, grad_heads, row_peak, row_sum):
-    seq_len = logits_full.shape[0]
-    head_count = logits_full.shape[1]
-    seq_count = value_heads.shape[0]
-    head_dim = value_heads.shape[3]
-    block_rows = min(512, seq_len)
-    blocks = seq_len // block_rows
-    logit_blocks = logits_full.reshape(blocks, block_rows, head_count, seq_len)
-    query_blocks = query_valid.reshape(seq_count, blocks, block_rows).transpose(1, 0, 2)
-    grad_blocks = grad_heads.reshape(seq_count, blocks, block_rows, head_count, head_dim).transpose(
-        1, 0, 2, 3, 4
-    )
-
-    def one_block(carried, operands):
-        logit_rows, grad_rows, query_rows, peak_rows, sum_rows = operands
-        scores = masked_scores(logit_rows, key_valid)
-        probabilities = jnp.exp(scores - peak_rows) / sum_rows
-        grad_masked = grad_rows * query_rows[:, :, None, None].astype(jnp.bfloat16)
-        dprobs = jnp.einsum(
-            "sqhd,skhd->sqhk", grad_masked, value_heads, preferred_element_type=jnp.float32
-        )
-        carried = carried + jnp.einsum(
-            "sqhk,sqhd->skhd",
-            probabilities.astype(jnp.bfloat16),
-            grad_masked,
-            preferred_element_type=jnp.float32,
-        )
-        dscores = probabilities * (dprobs - jnp.sum(probabilities * dprobs, axis=-1, keepdims=True))
-        return (carried, jnp.sum(dscores, axis=0))
-
-    zero_values = jnp.zeros(value_heads.shape, jnp.float32)
-    dvalue_heads, dlogit_blocks = lax.scan(
-        one_block, zero_values, (logit_blocks, grad_blocks, query_blocks, row_peak, row_sum)
-    )
-    return (dvalue_heads, dlogit_blocks.reshape(seq_len, head_count, seq_len))
+def weights_of(logit_rows, length_all):
+    seq_len = logit_rows.shape[2]
+    key_valid = (jnp.arange(seq_len)[None, :] < length_all[:, None]).astype(jnp.bfloat16)
+    terms = jnp.exp(logit_rows.astype(jnp.float32)).astype(jnp.bfloat16)
+    sums = jnp.einsum("phk,sk->sph", terms, key_valid, preferred_element_type=jnp.float32)
+    return (terms, sums, key_valid)
+
+
+def attend(terms, sums, value_all, query_rows):
+    mixed = jnp.einsum("phk,skhd->sphd", terms, value_all, preferred_element_type=jnp.float32)
+    mixed = mixed / sums[..., None]
+    return (mixed, (mixed * query_rows[:, :, None, None]).astype(jnp.bfloat16))
+
+
+def attend_back(terms, sums, key_valid, value_all, mixed, grad_rows):
+    along = jnp.sum(grad_rows.astype(jnp.float32) * mixed, axis=-1) / sums
+    scaled = (grad_rows.astype(jnp.float32) / sums[..., None]).astype(jnp.bfloat16)
+    dvalue_part = jnp.einsum("phk,sphd->skhd", terms, scaled, preferred_element_type=jnp.float32)
+    dlogits = jnp.einsum("sphd,skhd->phk", scaled, value_all, preferred_element_type=jnp.float32)
+    high = along.astype(jnp.bfloat16)
+    rest = (along - high.astype(jnp.float32)).astype(jnp.bfloat16)
+    shift = sum(
+        jnp.einsum("sph,sk->phk", part, key_valid, preferred_element_type=jnp.float32)
+        for part in (high, rest)
+    )
+    return (dvalue_part, terms.astype(jnp.float32) * (dlogits - shift))
 
 
 def on_device(
@@ -149,9 +110,17 @@
     positions = jnp.arange(seq_len)
     key_valid = positions[None, :] < seq_lengths[:, None]
     query_valid = key_valid.astype(jnp.float32)
-    logits_full = lax.all_gather(synth_logits, "ta", axis=0, tiled=True)
-    mixed_rows, row_peak, row_sum = attend(logits_full, value_heads, key_valid, query_valid)
-    attended = mixed_rows.reshape(rows_dev, local_width).astype(jnp.bfloat16)
+    length_all = lax.all_gather(seq_lengths, "ta", axis=0, tiled=True)
+    block_rows = synth_logits.shape[0]
+    value_all = lax.all_gather(
+        value_heads * key_valid[:, :, None, None].astype(jnp.bfloat16), "ta", axis=0, tiled=True
+    )
+    terms, sums, key_valid_all = weights_of(synth_logits, length_all)
+    block_positions = lax.axis_index("ta") * block_rows + jnp.arange(block_rows)
+    query_rows = (block_positions[None, :] < length_all[:, None]).astype(jnp.float32)
+    mixed_rows, mixed_low = attend(terms, sums, value_all, query_rows)
+    attended = lax.all_to_all(mixed_low, "ta", split_axis=0, concat_axis=1, tiled=True)
+    attended = attended.reshape(rows_dev, local_width)
     branch = (
         feature_share(jnp.dot(attended, out_rows, preferred_element_type=jnp.float32)) + out_bias
     )
@@ -196,10 +165,14 @@
     )
     out_bias_part = jnp.sum(dbranch.astype(jnp.float32), axis=0)
     grad_heads = dattended.reshape(seq_count, seq_len, head_count, head_dim)
-    dvalue_heads, logits_part = attend_back(
-        logits_full, value_heads, key_valid, query_valid, grad_heads, row_peak, row_sum
-    )
-    dvalues = dvalue_heads.reshape(rows_dev, local_width).astype(jnp.bfloat16)
+    grad_heads = grad_heads * query_valid[:, :, None, None].astype(jnp.bfloat16)
+    grad_block = lax.all_to_all(grad_heads, "ta", split_axis=1, concat_axis=0, tiled=True)
+    dvalue_part, logits_grad = attend_back(
+        terms, sums, key_valid_all, value_all, mixed_rows, grad_block
+    )
+    dvalue_rows = dvalue_part.astype(jnp.bfloat16).reshape(-1, local_width)
+    dvalue_rows = lax.psum_scatter(dvalue_rows, "ta", scatter_dimension=0, tiled=True)
+    dvalues = dvalue_rows * query_valid.reshape(rows_dev, 1).astype(jnp.bfloat16)
     value_part = lax.dot_general(layer_one, dvalues, ALONG_ROWS, preferred_element_type=jnp.float32)
     value_bias_part = jnp.sum(dvalues.astype(jnp.float32), axis=0)
     dlayer_one = feature_share(
@@ -212,12 +185,11 @@
         lax.all_to_all(up_part, "wa", split_axis=1, concat_axis=0, tiled=True),
         lax.all_to_all(down_part, "wa", split_axis=1, concat_axis=0, tiled=True),
     )
-    value_grad, out_grad, up_grad, down_grad, logits_grad = (
+    value_grad, out_grad, up_grad, down_grad = (
         lax.psum_scatter(value_part, "ta", scatter_dimension=0, tiled=True),
         lax.psum_scatter(out_part, "ta", scatter_dimension=1, tiled=True),
         lax.psum_scatter(up_back, "ta", scatter_dimension=0, tiled=True),
         lax.psum_scatter(down_back, "ta", scatter_dimension=0, tiled=True),
-        lax.psum_scatter(logits_part, "ta", scatter_dimension=0, tiled=True),
     )
     vector_grads = lax.psum(
         (

time: 1710 us -> 1020 us (0.60)
  waiting for transfers between devices: 1140 us -> 562 us
  other arithmetic: 112 us -> 29 us
  matrix products: 142 us -> 88.5 us
  blocking collectives: 221 us -> 251 us
    reduce_scatter x1, waiting for transfers between devices: 484 us -> 63.5 us  [on_device(): lax.psum_scatter(dvalue_rows, 'ta', scatter_dimension=0, tiled=True)]
    all_gather x1, waiting for transfers between devices: 219 us -> 47 us  [on_device(): lax.all_gather(value_heads * key_valid[:, :, None, None].astype(jnp.bfloa...]
    dot_general x12 -> x6, matrix products: 78.2 us -> 22.9 us  [the longest x1 6.7 us: attend(): jnp.einsum('phk,skhd->sphd', terms, value_all, preferred_element_type=jnp...]
    dynamic_update_slice x4 -> x0, other arithmetic: 46.6 us -> none  [attend_back(): lax.scan(one_block, zero_values, (logit_blocks, grad_blocks, query_blocks...]
    all_to_all x0 -> x1, blocking collectives: none -> 25.9 us  [on_device(): lax.all_to_all(grad_heads, 'ta', split_axis=1, concat_axis=0, tiled=True)]
    all_to_all x1, blocking collectives: 54.6 us -> 36.5 us  [on_device(): lax.all_to_all(down_part, 'wa', split_axis=1, concat_axis=0, tiled=True)]
    reduce_sum x4 -> x1, other arithmetic: 20.2 us -> 2.52 us  [attend_back(): along = jnp.sum(grad_rows.astype(jnp.float32) * mixed, axis=-1) / sums]
    unnamed x87 -> x92, local copies, waits for them, and re-layouts: 29.6 us -> 34.8 us
  transfers between devices with their start and end apart: 18 -> 19, of which waited for: 14 -> 14; matrix products, arithmetic and copies ran while one was open for 10% -> 9% of each run, Pallas kernels for 0% -> 0%
where the time goes in v1:
time: 1020 us
  waiting for transfers between devices  562 us (55%)
  blocking collectives  251 us (25%)
  matrix products  88.5 us (9%)
  local copies, waits for them, and re-layouts  55.8 us (5%)
  other arithmetic  29 us (3%)
  between operations  15.6 us (2%)
  starting transfers between devices  13.7 us (1%)
    reduce_scatter x4, waiting for transfers between devices, feature_share(): return lax.psum_scatter(partial_sum, 'wa', scatter_dimension=1, tiled=True)  193 us
    all_gather x4, waiting for transfers between devices, all_features(): return lax.all_gather(features_part, 'wa', axis=1, tiled=True)  156 us
    psum x4, blocking collectives, row_statistics(): lax.psum((jnp.sum(first_term, axis=1), jnp.sum(second_term, axis=1)), 'wa')  64.2 us
    reduce_scatter x1, waiting for transfers between devices, on_device(): lax.psum_scatter(dvalue_rows, 'ta', scatter_dimension=0, tiled=True)  63.5 us
    all_gather x1, waiting for transfers between devices, on_device(): lax.all_gather(value_heads * key_valid[:, :, None, None].astype(jnp.bfloa...  47 us
    all_to_all x1, blocking collectives, on_device(): lax.all_to_all(up_part, 'wa', split_axis=1, concat_axis=0, tiled=True)  44.3 us
    reduce_scatter x1, waiting for transfers between devices, on_device(): lax.psum_scatter(up_back, 'ta', scatter_dimension=0, tiled=True)  38.5 us
    all_to_all x1, blocking collectives, on_device(): lax.all_to_all(down_part, 'wa', split_axis=1, concat_axis=0, tiled=True)  36.5 us
  transfers between devices with their start and end apart: 19, of which 14 were waited for; matrix products, arithmetic and copies ran while one was open for 9% of the time, Pallas kernels for 0%

profile of v1, /device:TPU:0, one launch (start us, length us, event | category | flops | bytes accessed | tf_op | source)
XLA Modules:
  0.0 1016.0 jit_solution(7256846951548036443)
XLA Ops:
  9.9 17.5 %all-reduce.5 = (f32[2048]{0:T(1024)S(1)}, f32[2048]{0:T(1024)S(1)}) all-reduce(f32[2048]{0:T(1024)S(1)} %fusion.30, f32[2048]{0:T(1024)S(1)} %convert_reduce_fusion.2), channel_id=1, replica_groups=mesh['wa'=4,'ta'=8] {'wa'}, use_global_device_ids=true, to_apply=%region_3.0 | all-reduce | flops 4096 | bytes 32768 | tf_op jit(solution)/shard_map/psum | solution.py:15
  29.4 14.9 %all_gather.31 = bf16[768,192]{1,0:T(8,128)(2,1)S(1)} all-gather(bf16[96,192]{1,0:T(8,128)(2,1)S(1)} %copy-done.19), channel_id=1, replica_groups=mesh['wa'=4,'ta'=8] {'ta'}, dimensions={0}, use_global_device_ids=true | all-gather | bytes 331776 | tf_op jit(solution)/shard_map/all_gather | solution.py:94
  44.3 27.9 %all-gather.8.cloned.1.call-done = bf16[2048,768]{0,1:T(8,128)(2,1)} async-done(((bf16[2048,192]{0,1:T(8,128)(2,1)}), bf16[2048,768]{0,1:T(8,128)(2,1)}) %all-gather.8.cloned.1.call-update) | async-done | bytes 3145744 | tf_op jit(solution)/shard_map/all_gather | solution.py:19
  77.3 8.9 all-reduce
  93.8 47.0 %all-gather.10.cloned.1.call-done = bf16[8,2048,3,64]{1,3,0,2:T(8,128)(2,1)} async-done(((bf16[1,2048,3,64]{1,3,0,2:T(8,128)(2,1)}), bf16[8,2048,3,64]{1,3,0,2:T(8,128)(2,1)}) %all-gather.10.cloned.1.call-update) | async-done | bytes 6291472 | tf_op jit(solution)/shard_map/all_gather | solution.py:115
  140.8 6.7 multiply_convert_fusion.1
  152.2 27.9 %all_gather.34 = bf16[192,768]{0,1:T(8,128)(2,1)S(1)} all-gather(bf16[192,96]{0,1:T(8,128)(2,1)S(1)} %copy.97), channel_id=1, replica_groups=mesh['wa'=4,'ta'=8] {'ta'}, dimensions={1}, use_global_device_ids=true | all-gather | bytes 331776 | tf_op jit(solution)/shard_map/all_gather | solution.py:95
  185.8 69.8 %reduce-scatter.12.cloned.1.call-done = f32[2048,192]{0,1:T(8,128)} async-done(((f32[2048,768]{0,1:T(8,128)}), f32[2048,192]{0,1:T(8,128)}) %reduce-scatter.12.cloned.1.call-update) | async-done | bytes 1572880 | tf_op jit(solution)/shard_map/reduce_scatter | solution.py:23
  257.4 15.1 %all-reduce.4 = (f32[2048]{0:T(1024)S(1)}, f32[2048]{0:T(1024)S(1)}) all-reduce(f32[2048]{0:T(1024)S(1)} %get-tuple-element.99, f32[2048]{0:T(1024)S(1)} %get-tuple-element.98), channel_id=1, replica_groups=mesh['wa'=4,'ta'=8] {'wa'}, use_global_device_ids=true, to_apply=%region_8.0 | all-reduce | flops 4096 | bytes 32768 | tf_op jit(solution)/shard_map/psum | solution.py:15
  286.7 17.5 %all-gather.16.cloned.1.call-done = bf16[3072,192]{0,1:T(8,128)(2,1)} async-done(((bf16[384,192]{0,1:T(8,128)(2,1)}), bf16[3072,192]{0,1:T(8,128)(2,1)}) %all-gather.16.cloned.1.call-update) | async-done | bytes 1179664 | tf_op jit(solution)/shard_map/all_gather | solution.py:97
  311.4 47.0 %all-gather.12.cloned.1.call-done = bf16[2048,768]{0,1:T(8,128)(2,1)} async-done(((bf16[2048,192]{0,1:T(8,128)(2,1)}), bf16[2048,768]{0,1:T(8,128)(2,1)}) %all-gather.12.cloned.1.call-update) | async-done | bytes 3145744 | tf_op jit(solution)/shard_map/all_gather | solution.py:19
  358.4 7.6 fusion.59
  366.1 38.2 %all-gather.18.cloned.1.call-done = bf16[2048,768]{0,1:T(8,128)(2,1)} async-done(((bf16[2048,192]{0,1:T(8,128)(2,1)}), bf16[2048,768]{0,1:T(8,128)(2,1)}) %all-gather.18.cloned.1.call-update) | async-done | bytes 3145744 | tf_op jit(solution)/shard_map/all_gather | solution.py:19
  404.3 11.5 %convert_reduce_fusion = (f32[768]{0:T(1024)}, bf16[2048,768]{1,0:T(8,128)(2,1)S(1)}, bf16[2048,768]{1,0:T(8,128)(2,1)}) fusion(f32[2048,768]{1,0:T(8,128)} %fusion.59, f32[768]{0:T(1024)S(1)} %copy-done.36, bf16[2048,768]{0,1:T(8,128)(2,1)} %all-gather.18.cloned.1.call-done, bf16[768,768]{0,1:T(8,128)(2,1)} %bitcast.12), kind=kOutput, calls=%fused_computation.11 | convolution fusion | flops 2455239936 | bytes 16914432 | tf_op jit(solution)/shard_map/dot_general | solution.py:144
  417.4 5.8 fusion.61
  423.3 70.3 %reduce-scatter.16.cloned.1.call-done = f32[2048,192]{0,1:T(8,128)} async-done(((f32[2048,768]{0,1:T(8,128)}), f32[2048,192]{0,1:T(8,128)}) %reduce-scatter.16.cloned.1.call-update) | async-done | bytes 1572880 | tf_op jit(solution)/shard_map/reduce_scatter | solution.py:23
  496.3 16.3 %all-reduce.3 = (f32[2048]{0:T(1024)}, f32[2048]{0:T(1024)}) all-reduce(f32[2048]{0:T(1024)} %get-tuple-element.91, f32[2048]{0:T(1024)} %get-tuple-element.95), channel_id=1, replica_groups=mesh['wa'=4,'ta'=8] {'wa'}, use_global_device_ids=true, to_apply=%region_14.0 | all-reduce | flops 4096 | bytes 32768 | tf_op jit(solution)/shard_map/psum | solution.py:15
  517.5 43.3 %all-gather.20.cloned.1.call-done = bf16[2048,768]{0,1:T(8,128)(2,1)} async-done(((bf16[2048,192]{0,1:T(8,128)(2,1)}), bf16[2048,768]{0,1:T(8,128)(2,1)}) %all-gather.20.cloned.1.call-update) | async-done | bytes 3145744 | tf_op jit(solution)/shard_map/all_gather | solution.py:19
  572.7 25.9 %all_to_all.94 = bf16[8,2,24576]{2,1,0:T(2,128)(2,1)} all-to-all(bf16[8,2,24576]{2,1,0:T(2,128)(2,1)} %reshape.189), channel_id=1, replica_groups=mesh['wa'=4,'ta'=8] {'ta'}, dimensions={0} | all-to-all | bytes 1572864 | tf_op jit(solution)/shard_map/all_to_all | solution.py:169
  616.0 7.0 copy.129
  627.4 63.5 %reduce-scatter.18.cloned.1.call-done = bf16[2048,192]{0,1:T(8,128)(2,1)} async-done(((bf16[16384,192]{0,1:T(8,128)(2,1)}), bf16[2048,192]{0,1:T(8,128)(2,1)}) %reduce-scatter.18.cloned.1.call-update) | async-done | bytes 786448 | tf_op jit(solution)/shard_map/reduce_scatter | solution.py:174
  695.7 7.5 fusion.60
  708.7 36.5 %all_to_all.95 = f32[768,4,192]{0,2,1:T(8,128)S(1)} all-to-all(f32[768,4,192]{0,2,1:T(8,128)S(1)} %bitcast.173), channel_id=1, replica_groups=mesh['wa'=4,'ta'=8] {'wa'}, dimensions={1} | all-to-all | bytes 4718592 | tf_op jit(solution)/shard_map/all_to_all | solution.py:186
  747.1 5.8 fusion.63
  752.9 44.3 %all_to_all.96 = f32[768,4,192]{0,2,1:T(8,128)S(1)} all-to-all(f32[768,4,192]{0,2,1:T(8,128)S(1)} %bitcast.174), channel_id=1, replica_groups=mesh['wa'=4,'ta'=8] {'wa'}, dimensions={1} | all-to-all | bytes 4718592 | tf_op jit(solution)/shard_map/all_to_all | solution.py:185
  805.0 5.7 fusion.53
  815.3 6.7 copy.110
  829.6 15.3 %all-reduce.2 = (f32[2048]{0:T(1024)S(1)}, f32[2048]{0:T(1024)S(1)}) all-reduce(f32[2048]{0:T(1024)S(1)} %get-tuple-element.93, f32[2048]{0:T(1024)S(1)} %get-tuple-element.94), channel_id=1, replica_groups=mesh['wa'=4,'ta'=8] {'wa'}, use_global_device_ids=true, to_apply=%region_20.0 | all-reduce | flops 4096 | bytes 32768 | tf_op jit(solution)/shard_map/psum | solution.py:15
  844.9 52.8 %reduce-scatter.14.cloned.1.call-done = f32[2048,192]{0,1:T(8,128)} async-done(((f32[2048,768]{0,1:T(8,128)}), f32[2048,192]{0,1:T(8,128)}) %reduce-scatter.14.cloned.1.call-update) | async-done | bytes 1572880 | tf_op jit(solution)/shard_map/reduce_scatter | solution.py:23
  903.1 28.8 %all-reduce.1 = (f32[192]{0:T(256)}, f32[192]{0:T(256)}, f32[192]{0:T(256)}, f32[192]{0:T(256)}, f32[192]{0:T(256)}, /*index=5*/f32[192]{0:T(256)}, f32[768]{0:T(1024)}, f32[192]{0:T(256)}) all-reduce(f32[192]{0:T(256)S(1)} %get-tuple-element.92, f32[192]{0:T(256)S(1)} %get-tuple-element.97, ...), channel_id=1, replica_groups=mesh['wa'=4,'ta'=8] {'ta'}, use_global_device_ids=true, to_apply=%region_22.0 | all-reduce | flops 2112 | bytes 16896 | tf_op jit(solution)/shard_map/psum | solution.py:194
  937.1 38.5 %reduce-scatter.24.cloned.1.call-done = f32[384,192]{0,1:T(8,128)} async-done(((f32[3072,192]{0,1:T(8,128)}), f32[384,192]{0,1:T(8,128)}) %reduce-scatter.24.cloned.1.call-update) | async-done | bytes 294928 | tf_op jit(solution)/shard_map/reduce_scatter | solution.py:191
  975.5 33.5 %reduce-scatter.22.cloned.1.call-done = f32[96,192]{1,0:T(8,128)} async-done(((f32[768,192]{1,0:T(8,128)}), f32[96,192]{1,0:T(8,128)}) %reduce-scatter.22.cloned.1.call-update) | async-done | bytes 73744 | tf_op jit(solution)/shard_map/reduce_scatter | solution.py:189
  (174 shorter events, 135.3 us)
Async XLA Ops:
  7.2 20.3 %copy-start = (bf16[192,2048]{1,0:T(8,128)(2,1)S(1)}, bf16[192,2048]{1,0:T(8,128)(2,1)}, u32[]{:S(2)}) copy-start(bf16[192,2048]{1,0:T(8,128)(2,1)} %param.16) | copy-start | bytes 2359300
  7.2 65.0 %all-gather.8.cloned.1.call-start = ((), (), s32[]{:S(2)}) async-start(), calls=%async_computation.15 | async-start | bytes 3932160 | tf_op jit(solution)/shard_map/all_gather | solution.py:19
  8.6 20.8 %copy-start.19 = (bf16[96,192]{1,0:T(8,128)(2,1)S(1)}, bf16[96,192]{1,0:T(8,128)(2,1)}, u32[]{:S(2)}) copy-start(bf16[96,192]{1,0:T(8,128)(2,1)} %param.20) | copy-start | bytes 110596
  9.9 62.3 %copy-start.37 = (f32[192]{0:T(256)S(1)}, f32[192]{0:T(256)}, u32[]{:S(2)}) copy-start(f32[192]{0:T(256)} %param.21) | copy-start | bytes 2308
  28.7 112.1 %all-gather.10.cloned.1.call-start = ((), (), s32[]{:S(2)}) async-start(), calls=%async_computation.16 | async-start | bytes 7077888 | tf_op jit(solution)/shard_map/all_gather | solution.py:115
  93.8 53.7 %copy-start.8 = (f32[8,256,3]{1,0,2:T(8,128)}, f32[8,256,3]{1,0,2:T(8,128)S(1)}, u32[]{:S(2)}) copy-start(f32[8,256,3]{1,0,2:T(8,128)S(1)} %fusion.12) | copy-start | bytes 73732
  148.5 31.7 %all-to-all-start = ((bf16[8,256,3,64]{1,3,2,0:T(8,128)(2,1)}), bf16[8,256,3,64]{1,3,2,0:T(8,128)(2,1)S(1)}, u32[]{:S(2)}, u32[]{:S(2)}) async-start(bf16[8,256,3,64]{1,3,2,0:T(8,128)(2,1)} %copy.95), calls=%async_computation | async-start | bytes 1572864 | tf_op jit(solution)/shard_map/all_to_all | solution.py:122
  152.0 103.6 %reduce-scatter.12.cloned.1.call-start = ((), (), s32[]{:S(2)}) async-start(), calls=%async_computation.17 | async-start | bytes 7864320 | tf_op jit(solution)/shard_map/reduce_scatter | solution.py:23
  184.5 71.0 %copy-start.33 = (f32[192]{0:T(256)S(1)}, f32[192]{0:T(256)}, u32[]{:S(2)}) copy-start(f32[192]{0:T(256)} %param.24) | copy-start | bytes 2308
  184.6 95.5 %all-gather.14.cloned.1.call-start = ((), (), s32[]{:S(2)}) async-start(), calls=%async_computation.19 | async-start | bytes 1327104 | tf_op jit(solution)/shard_map/all_gather | solution.py:96
  185.2 119.1 %all-gather.16.cloned.1.call-start = ((), (), s32[]{:S(2)}) async-start(), calls=%async_computation.20 | async-start | bytes 1327104 | tf_op jit(solution)/shard_map/all_gather | solution.py:97
  185.7 86.8 %copy-start.22 = (f32[192]{0:T(256)S(1)}, f32[192]{0:T(256)}, u32[]{:S(2)}) copy-start(f32[192]{0:T(256)} %param.25) | copy-start | bytes 2308
  185.8 86.8 %copy-start.34 = (f32[192]{0:T(256)S(1)}, f32[192]{0:T(256)}, u32[]{:S(2)}) copy-start(f32[192]{0:T(256)} %param.26) | copy-start | bytes 2308
  185.8 172.7 %all-gather.12.cloned.1.call-start = ((), (), s32[]{:S(2)}) async-start(), calls=%async_computation.18 | async-start | bytes 3932160 | tf_op jit(solution)/shard_map/all_gather | solution.py:19
  273.8 130.5 %all-gather.18.cloned.1.call-start = ((), (), s32[]{:S(2)}) async-start(), calls=%async_computation.22 | async-start | bytes 3932160 | tf_op jit(solution)/shard_map/all_gather | solution.py:19
  282.4 24.2 %all-to-all-start.1 = ((bf16[4,768,192]{1,2,0:T(8,128)(2,1)}), bf16[4,768,192]{1,2,0:T(8,128)(2,1)}, u32[]{:S(2)}, u32[]{:S(2)}) async-start(bf16[4,768,192]{1,2,0:T(8,128)(2,1)} %bitcast.154), calls=%async_computation.2 | async-start | bytes 2359296 | tf_op jit(solution)/shard_map/all_to_all | solution.py:100
  306.6 59.4 %all-to-all-start.2 = ((bf16[4,768,192]{1,2,0:T(8,128)(2,1)}), bf16[4,768,192]{1,2,0:T(8,128)(2,1)}, u32[]{:S(2)}, u32[]{:S(2)}) async-start(bf16[4,768,192]{1,2,0:T(8,128)(2,1)} %bitcast.153), calls=%async_computation.3 | async-start | bytes 2359296 | tf_op jit(solution)/shard_map/all_to_all | solution.py:101
  310.9 182.7 %reduce-scatter.16.cloned.1.call-start = ((), (), s32[]{:S(2)}) async-start(), calls=%async_computation.23 | async-start | bytes 7864320 | tf_op jit(solution)/shard_map/reduce_scatter | solution.py:23
  358.4 45.9 %copy-start.36 = (f32[768]{0:T(1024)S(1)}, f32[768]{0:T(1024)}, u32[]{:S(2)}) copy-start(f32[768]{0:T(1024)} %param.28) | copy-start | bytes 9220
  423.2 90.1 %copy-start.3 = (bf16[192,2048]{1,0:T(8,128)(2,1)S(1)}, bf16[192,2048]{1,0:T(8,128)(2,1)}, u32[]{:S(2)}) copy-start(bf16[192,2048]{1,0:T(8,128)(2,1)} %param.31) | copy-start | bytes 2359300
  423.2 137.6 %all-gather.20.cloned.1.call-start = ((), (), s32[]{:S(2)}) async-start(), calls=%async_computation.24 | async-start | bytes 3932160 | tf_op jit(solution)/shard_map/all_gather | solution.py:19
  516.9 174.0 %reduce-scatter.18.cloned.1.call-start = ((), (), s32[]{:S(2)}) async-start(), calls=%async_computation.25 | async-start | bytes 7077888 | tf_op jit(solution)/shard_map/reduce_scatter | solution.py:174
  623.0 176.3 %reduce-scatter.28.cloned.1.call-start = ((), (), s32[]{:S(2)}) async-start(), calls=%async_computation.30 | async-start | bytes 884736
  627.3 200.2 %reduce-scatter.20.cloned.1.call-start = ((), (), s32[]{:S(2)}) async-start(), calls=%async_computation.26 | async-start | bytes 7864320 | tf_op jit(solution)/shard_map/reduce_scatter | solution.py:23
  695.6 202.1 %reduce-scatter.14.cloned.1.call-start = ((), (), s32[]{:S(2)}) async-start(), calls=%async_computation.21 | async-start | bytes 7864320 | tf_op jit(solution)/shard_map/reduce_scatter | solution.py:23
  703.2 233.9 %reduce-scatter.26.cloned.1.call-start = ((), (), s32[]{:S(2)}) async-start(), calls=%async_computation.29 | async-start | bytes 2654208 | tf_op jit(solution)/shard_map/reduce_scatter | solution.py:192
  747.1 228.5 %reduce-scatter.24.cloned.1.call-start = ((), (), s32[]{:S(2)}) async-start(), calls=%async_computation.28 | async-start | bytes 2654208 | tf_op jit(solution)/shard_map/reduce_scatter | solution.py:191
  799.0 210.0 %reduce-scatter.22.cloned.1.call-start = ((), (), s32[]{:S(2)}) async-start(), calls=%async_computation.27 | async-start | bytes 884736 | tf_op jit(solution)/shard_map/reduce_scatter | solution.py:189
  826.0 71.7 %copy-start.16 = (f32[2048]{0:T(1024)S(1)}, f32[2048]{0:T(1024)}, u32[]{:S(2)}) copy-start(f32[2048]{0:T(1024)} %copy-done.15) | copy-start | bytes 24580
  826.0 71.7 %copy-start.21 = (f32[2048]{0:T(1024)S(1)}, f32[2048]{0:T(1024)}, u32[]{:S(2)}) copy-start(f32[2048]{0:T(1024)} %get-tuple-element.110) | copy-start | bytes 24580
  826.1 71.7 %copy-start.23 = (f32[192]{0:T(256)S(1)}, f32[192]{0:T(256)}, u32[]{:S(2)}) copy-start(f32[192]{0:T(256)} %param.25) | copy-start | bytes 2308
  826.1 71.7 %copy-start.35 = (f32[192]{0:T(256)S(1)}, f32[192]{0:T(256)}, u32[]{:S(2)}) copy-start(f32[192]{0:T(256)} %param.30) | copy-start | bytes 2308
  (27 other events, 150.6 us)
Sparse Core Ops, SparseCore 0:
  28.8 43.3 all-gather.7
  76.0 64.7 all-gather.9
  184.7 70.8 reduce-scatter.11
  257.1 22.9 all-gather.13
  281.5 22.6 all-gather.15
  306.5 51.8 all-gather.11
  360.3 43.9 all-gather.17
  423.3 70.2 reduce-scatter.15
  517.0 43.7 all-gather.19
  623.2 67.7 reduce-scatter.17
  693.8 29.8 reduce-scatter.27
  726.8 97.1 reduce-scatter.19
  827.3 70.3 reduce-scatter.13
  900.6 36.4 reduce-scatter.25
  939.9 35.5 reduce-scatter.23
  978.4 30.6 reduce-scatter.21

commit v2 on v1

--- a/solution.py
+++ b/solution.py
@@ -1,6 +1,10 @@
+import functools
+
 import jax
 import jax.numpy as jnp
 from jax import lax
+from jax.experimental import pallas as pl
+from jax.experimental.pallas import tpu as pltpu
 from jax.sharding import PartitionSpec as P
 
 D = 768
@@ -223,6 +227,1348 @@
     )
 
 
+MESH = pl.DeviceIdType.MESH
+ROWS_NT = (((1,), (1,)), ((), ()))
+ROWS_TN = (((0,), (0,)), ((), ()))
+F32 = jnp.float32
+BF16 = jnp.bfloat16
+VMEM_BYTES = 60 * 2**20
+CHUNK = 128
+PAD = 128
+
+
+def whole(count):
+    return [pl.BlockSpec(memory_space=pltpu.VMEM)] * count
+
+
+def anywhere(count):
+    return [pl.BlockSpec(memory_space=pl.ANY)] * count
+
+
+def shape_of(shape, dtype):
+    return jax.ShapeDtypeStruct(shape, dtype)
+
+
+def lanes(start, size=CHUNK):
+    return pl.ds(pl.multiple_of(start, CHUNK), size)
+
+
+def rows_at(start, size, unit):
+    return pl.ds(pl.multiple_of(start, unit), size)
+
+
+class Place:
+    def __init__(self, nwa, nta):
+        self.nwa, self.nta, self.nz = nwa, nta, nta // 2
+        self.wa = lax.axis_index("wa")
+        self.ta = lax.axis_index("ta")
+        self.z = self.ta // 2
+        self.c = self.ta % 2
+        self.peer = self.ta + 1 - 2 * self.c
+        self.wx = self.wa + 1 - 2 * (self.wa % 2)
+        self.wy = (self.wa + 2) % 4
+        self.wd = 3 - self.wa
+
+    def enter(self):
+        barrier = pltpu.get_barrier_semaphore()
+        total = self.nwa * self.nta
+
+        def greet(step, carry):
+            w = (self.wa + step // self.nta) % self.nwa
+            t = (self.ta + step % self.nta) % self.nta
+            pl.semaphore_signal(barrier, inc=1, device_id=(w, t), device_id_type=MESH)
+            return carry
+
+        lax.fori_loop(1, total, greet, 0)
+        pl.semaphore_wait(barrier, total - 1)
+
+
+def send(src, dst, ssem, rsem, device):
+    return pltpu.make_async_remote_copy(
+        src_ref=src,
+        dst_ref=dst,
+        send_sem=ssem,
+        recv_sem=rsem,
+        device_id=device,
+        device_id_type=MESH,
+    )
+
+
+def when(condition):
+    return pl.when(condition)
+
+
+def norm_stats(block):
+    width = block.shape[0]
+    mean = jnp.sum(block, axis=0, keepdims=True) / width
+    centred = block - mean
+    variance = jnp.sum(centred * centred, axis=0, keepdims=True) / width
+    inverse = lax.rsqrt(variance + EPSILON)
+    return (centred * inverse, inverse)
+
+
+def forward_kernel(
+    dims,
+    tok,
+    cot,
+    wp,
+    pcol,
+    prow,
+    ln,
+    logits,
+    xown,
+    cown,
+    attended,
+    weights,
+    layer_out,
+    value_out,
+    term_out,
+    mixed,
+    zinv,
+    lens,
+    pfull,
+    rfull,
+    x,
+    wvc,
+    layer_pad,
+    layer,
+    value,
+    terms,
+    attsend,
+    sem_tok,
+    sem_par,
+    sem_ta,
+    sem_val,
+    sem_w,
+    sem_cot,
+    sem_att,
+    sem_local,
+):
+    nwa, nta = dims
+    me = Place(nwa, nta)
+    wa, ta, z, c = me.wa, me.ta, me.z, me.c
+    nz = me.nz
+    width = tok.shape[0]
+    half = width // 2
+    seq = tok.shape[1]
+    part = seq // nz
+    query = seq // nta
+    slot = wvc.shape[1] // nta
+    wdepth = wvc.shape[0] * nwa // nta
+    heads = logits.shape[0]
+    hdim = width // heads
+    split = wp.shape[1] - PAD
+    me.enter()
+    done = []
+
+    def block_rows(w, off=0, size=width):
+        return rows_at(w * width + off, size, 32)
+
+    def tok_copy(k, q):
+        device = (me.wx if k == 0 else me.wy, ta)
+        return send(
+            tok.at[:, pl.ds(q * part, part)],
+            x.at[block_rows(wa), pl.ds(q * part, part)],
+            sem_tok.at[0, k, q],
+            sem_tok.at[1, k, q],
+            device,
+        )
+
+    def tok_fwd(k, q):
+        source = me.wx if k == 0 else me.wy
+        device = (me.wy if k == 0 else me.wx, ta)
+        where = x.at[block_rows(source, k * half, half), pl.ds(q * part, part)]
+        return send(where, where, sem_tok.at[0, 2 + k, q], sem_tok.at[1, 2 + k, q], device)
+
+    own_x = pltpu.make_async_copy(tok, x.at[block_rows(wa)], sem_local.at[0])
+    own_x.start()
+    for q in range(nz):
+        for k in range(2):
+            tok_copy(k, q).start()
+
+    def par_copy(step, what):
+        w = (wa + step) % nwa
+        if what == 0:
+            src, dst = pcol, pfull.at[block_rows(wa)]
+        else:
+            src, dst = prow, rfull.at[:, lanes(wa * prow.shape[1], prow.shape[1])]
+        return send(src, dst, sem_par.at[0, what, step], sem_par.at[1, what, step], (w, ta))
+
+    def ta_copy(step, what):
+        t = (ta + step) % nta
+        if what == 0:
+            src, dst = wp.at[:, pl.ds(split, PAD)], wvc.at[:, lanes(ta * slot)]
+        else:
+            src, dst = ln, lens.at[rows_at(ta * 8, 8, 8)]
+        return send(src, dst, sem_ta.at[0, what, step], sem_ta.at[1, what, step], (wa, t))
+
+    for step in range(1, nta):
+        ta_copy(step, 0).start()
+        ta_copy(step, 1).start()
+    for step in range(1, nwa):
+        par_copy(step, 0).start()
+        par_copy(step, 1).start()
+    own_wv = pltpu.make_async_copy(
+        wp.at[:, pl.ds(split, PAD)], wvc.at[:, lanes(ta * slot)], sem_local.at[1]
+    )
+    own_wv.start()
+    pfull[block_rows(wa), :] = pcol[...]
+    rfull[:, lanes(wa * prow.shape[1], prow.shape[1])] = prow[...]
+    lens[rows_at(ta * 8, 8, 8), :] = ln[...]
+
+    own_w = pltpu.make_async_copy(wp, weights.at[wa, ta], sem_local.at[2])
+    own_w.start()
+
+    def w_line(up, b, own):
+        t = 2 * b + c
+        where = weights.at[wa, t]
+        k = 0 if up else 1
+        return send(
+            wp if own else where,
+            where,
+            sem_w.at[0, k, b],
+            sem_w.at[1, k, b],
+            (wa, ta + 2 if up else ta - 2),
+        )
+
+    @pl.when(z < nz - 1)
+    def _():
+        w_line(True, z, True).start()
+
+    @pl.when(z > 0)
+    def _():
+        w_line(False, z, True).start()
+
+    layer_pad[...] = jnp.zeros_like(layer_pad)
+    for h in range(heads):
+        terms[h] = jnp.exp(logits[h].astype(F32)).astype(BF16)
+    out_terms = pltpu.make_async_copy(terms, term_out, sem_local.at[3])
+    out_terms.start()
+
+    own_wv.wait()
+    for step in range(1, nta):
+        ta_copy(step, 0).wait_recv()
+        ta_copy(step, 1).wait_recv()
+    for step in range(1, nwa):
+        par_copy(step, 0).wait_recv()
+        par_copy(step, 1).wait_recv()
+    own_x.wait()
+
+    positions = lax.broadcasted_iota(jnp.int32, (nta * 8, seq), 1).astype(F32)
+    key_valid = jnp.where(positions < lens[:, 0:1], 1.0, 0.0).astype(BF16)
+    for h in range(heads):
+        sums = lax.dot_general(key_valid, terms[h], ROWS_NT, preferred_element_type=F32)
+        zinv[h] = 1.0 / sums
+
+    def value_copy(kind, b, q, core):
+        where = value.at[2 * b + core, :, pl.ds(q * part, part)]
+        t = (ta + 2, ta - 2, me.peer)[kind]
+        return send(where, where, sem_val.at[0, kind, b, q], sem_val.at[1, kind, b, q], (wa, t))
+
+    def w_hop(h):
+        @pl.when(z - 1 - h >= 0)
+        def _():
+            w_line(True, z - 1 - h, False).wait_recv()
+
+            @pl.when(z < nz - 1)
+            def _():
+                w_line(True, z - 1 - h, False).start()
+
+        @pl.when(z + 1 + h < nz)
+        def _():
+            w_line(False, z + 1 + h, False).wait_recv()
+
+            @pl.when(z > 0)
+            def _():
+                w_line(False, z + 1 + h, False).start()
+
+    for q in range(nz):
+        cols = pl.ds(q * part, part)
+        for k in range(2):
+            tok_copy(k, q).wait_recv()
+            tok_fwd(k, q).start()
+        for k in range(2):
+            where = x.at[block_rows(me.wd, k * half, half), cols]
+            send(
+                where,
+                where,
+                sem_tok.at[0, 2 + k, q],
+                sem_tok.at[1, 2 + k, q],
+                (me.wy if k == 0 else me.wx, ta),
+            ).wait_recv()
+        normed, _ = norm_stats(x[:, cols].astype(F32))
+        low = (normed * pfull[:, 0:1] + pfull[:, 1:2]).astype(BF16)
+        layer[:, cols] = low
+        for t in range(nta):
+            layer_pad[t * slot : t * slot + wdepth, :] = low[t * wdepth : (t + 1) * wdepth]
+        made = jnp.dot(wvc[...], layer_pad[...], preferred_element_type=F32) + pcol[:, 2:3]
+        place = lax.broadcasted_iota(jnp.int32, (width, part), 1) + q * part
+        made = jnp.where(place.astype(F32) < ln[0:1, 0:1], made, 0.0)
+        value[ta, :, cols] = made.astype(BF16)
+        xown[:, pl.ds(q * CHUNK, CHUNK)] = x[:, lanes(q * part + wa * CHUNK)]
+
+        @pl.when(z < nz - 1)
+        def _():
+            value_copy(0, z, q, c).start()
+
+        @pl.when(z > 0)
+        def _():
+            value_copy(1, z, q, c).start()
+
+        value_copy(2, z, q, c).start()
+        if q >= 1 and q - 1 < nz - 1:
+            w_hop(q - 1)
+    out_layer = pltpu.make_async_copy(layer, layer_out, sem_local.at[4])
+    out_layer.start()
+
+    def cot_copy(step, q):
+        w = (wa + step) % nwa
+        return send(
+            cot.at[:, lanes(q * part + w * CHUNK)],
+            cown.at[block_rows(wa), pl.ds(q * CHUNK, CHUNK)],
+            sem_cot.at[0, step, q],
+            sem_cot.at[1, step, q],
+            (w, ta),
+        )
+
+    def cot_own(q):
+        return pltpu.make_async_copy(
+            cot.at[:, lanes(q * part + wa * CHUNK)],
+            cown.at[block_rows(wa), pl.ds(q * CHUNK, CHUNK)],
+            sem_cot.at[0, 0, q],
+        )
+
+    own_w.wait()
+
+    def w_plane(k, b):
+        device = (me.wx if k == 0 else me.wy, ta)
+        where = weights.at[wa, 2 * b + c]
+        return send(where, where, sem_w.at[0, 2 + k, b], sem_w.at[1, 2 + k, b], device)
+
+    def w_diag(k, b, source):
+        device = (me.wy if k == 0 else me.wx, ta)
+        where = weights.at[source, 2 * b + c, pl.ds(k * half, half)]
+        return send(where, where, sem_w.at[0, 4 + k, b], sem_w.at[1, 4 + k, b], device)
+
+    def w_core(r, b, core):
+        source = (wa, me.wx, me.wy, me.wd)[r]
+        where = weights.at[source, 2 * b + core]
+        return send(where, where, sem_w.at[0, 6 + r, b], sem_w.at[1, 6 + r, b], (wa, me.peer))
+
+    for b in range(nz):
+        w_plane(0, b).start()
+        w_plane(1, b).start()
+        w_core(0, b, c).start()
+    for q in range(nz):
+        cot_own(q).start()
+        for step in range(1, nwa):
+            cot_copy(step, q).start()
+
+    def w_forward(b):
+        w_plane(0, b).wait_recv()
+        w_diag(0, b, me.wx).start()
+        w_core(1, b, c).start()
+        w_plane(1, b).wait_recv()
+        w_diag(1, b, me.wy).start()
+        w_core(2, b, c).start()
+
+    def w_finish(b):
+        for k in range(2):
+            w_diag(k, b, me.wd).wait_recv()
+        w_core(3, b, c).start()
+
+    def att_copy(s, j):
+        return send(
+            attsend.at[s, :, pl.ds(j * CHUNK, CHUNK)],
+            attended.at[block_rows(wa), lanes(z * CHUNK)],
+            sem_att.at[0, s, j],
+            sem_att.at[1, wa, z],
+            (2 * c + j, s),
+        )
+
+    def att_local(s, j):
+        return pltpu.make_async_copy(
+            attsend.at[s, :, pl.ds(j * CHUNK, CHUNK)],
+            attended.at[block_rows(wa), lanes(z * CHUNK)],
+            sem_att.at[0, s, j],
+        )
+
+    def is_self(s, j):
+        return jnp.logical_and(s == ta, 2 * c + j == wa)
+
+    def mix(b):
+        for core in range(2):
+            s = 2 * b + core
+            out_value = pltpu.make_async_copy(value.at[s], value_out.at[s], sem_local.at[6 + core])
+            out_value.start()
+        length = [lens[rows_at((2 * b + core) * 8, 8, 8), :][0:1, 0:1] for core in range(2)]
+        place = lax.broadcasted_iota(jnp.int32, (hdim, query), 1) + ta * query
+        place = place.astype(F32)
+        for h in range(heads):
+            group = slice(h * hdim, (h + 1) * hdim)
+            pair = jnp.concatenate([value[2 * b, group, :], value[2 * b + 1, group, :]], axis=0)
+            both = lax.dot_general(pair, terms[h], ROWS_NT, preferred_element_type=F32)
+            for core in range(2):
+                s = 2 * b + core
+                inverse = zinv[h, rows_at(s * 8, 8, 8), :][0:1]
+                one = both[core * hdim : (core + 1) * hdim] * inverse
+                mixed[s, group, :] = one
+                one = jnp.where(place < length[core], one, 0.0)
+                attsend[s, group, :] = one.astype(BF16)
+        for core in range(2):
+            s = 2 * b + core
+            for j in range(2):
+
+                @pl.when(is_self(s, j))
+                def _():
+                    att_local(s, j).start()
+
+                @pl.when(jnp.logical_not(is_self(s, j)))
+                def _():
+                    att_copy(s, j).start()
+
+            pltpu.make_async_copy(value.at[s], value_out.at[s], sem_local.at[6 + core]).wait()
+
+    def core_ready(b):
+        for q in range(nz):
+            value_copy(2, b, q, 1 - c).wait_recv()
+
+    for h in range(nz - 1):
+        below, above = z - 1 - h, z + 1 + h
+        for q in range(nz):
+
+            @pl.when(below >= 0)
+            def _():
+                value_copy(0, below, q, c).wait_recv()
+
+                @pl.when(z < nz - 1)
+                def _():
+                    value_copy(0, below, q, c).start()
+
+                value_copy(2, below, q, c).start()
+
+            @pl.when(above < nz)
+            def _():
+                value_copy(1, above, q, c).wait_recv()
+
+                @pl.when(z > 0)
+                def _():
+                    value_copy(1, above, q, c).start()
+
+                value_copy(2, above, q, c).start()
+
+        if h == 0:
+            core_ready(z)
+            mix(z)
+
+        @pl.when(below >= 0)
+        def _():
+            core_ready(below)
+            mix(below)
+
+        @pl.when(above < nz)
+        def _():
+            core_ready(above)
+            mix(above)
+
+        w_forward(h)
+    for b in range(nz - 1, nz):
+        w_forward(b)
+    for b in range(nz):
+        w_finish(b)
+
+    for step in range(1, nta):
+        ta_copy(step, 0).wait_send()
+        ta_copy(step, 1).wait_send()
+    for step in range(1, nwa):
+        par_copy(step, 0).wait_send()
+        par_copy(step, 1).wait_send()
+        for q in range(nz):
+            cot_copy(step, q).wait_send()
+    for q in range(nz):
+        cot_own(q).wait()
+        for k in range(2):
+            tok_copy(k, q).wait_send()
+            tok_fwd(k, q).wait_send()
+    for step in range(1, nwa):
+        for q in range(nz):
+            cot_copy(step, q).wait_recv()
+
+    def line_sends(b, carry):
+        reach_up = jnp.logical_and(b <= z, z < nz - 1)
+        reach_down = jnp.logical_and(b >= z, z > 0)
+
+        @pl.when(reach_up)
+        def _():
+            w_line(True, b, False).wait_send()
+            for q in range(nz):
+                value_copy(0, b, q, c).wait_send()
+
+        @pl.when(reach_down)
+        def _():
+            w_line(False, b, False).wait_send()
+            for q in range(nz):
+                value_copy(1, b, q, c).wait_send()
+
+        for q in range(nz):
+            value_copy(2, b, q, c).wait_send()
+        for k in range(2):
+            w_plane(k, b).wait_send()
+        w_diag(0, b, me.wx).wait_send()
+        w_diag(1, b, me.wy).wait_send()
+        for r in range(4):
+            w_core(r, b, c).wait_send()
+            w_core(r, b, 1 - c).wait_recv()
+        return carry
+
+    lax.fori_loop(0, nz, line_sends, 0)
+
+    def att_sends(s, carry):
+        for j in range(2):
+
+            @pl.when(is_self(s, j))
+            def _():
+                att_local(s, j).wait()
+
+            @pl.when(jnp.logical_not(is_self(s, j)))
+            def _():
+                att_copy(s, j).wait_send()
+
+        return carry
+
+    lax.fori_loop(0, nta, att_sends, 0)
+    mine = wa // 2
+
+    def att_arrivals(k, carry):
+        w, b = k // nz, k % nz
+
+        @pl.when(jnp.logical_not(jnp.logical_and(w == wa, 2 * b + mine == ta)))
+        def _():
+            where = attended.at[block_rows(w), lanes(b * CHUNK)]
+            send(where, where, sem_att.at[0, 0, 0], sem_att.at[1, w, b], (w, 2 * b + mine)).wait_recv()
+
+        return carry
+
+    lax.fori_loop(0, nwa * nz, att_arrivals, 0)
+    out_terms.wait()
+    out_layer.wait()
+
+
+def run_forward(dims, tok, cot, wp, pcol, prow, ln, logits):
+    nwa, nta = dims
+    nz = nta // 2
+    width, seq = tok.shape
+    depth = width * nwa
+    own = seq // nwa
+    heads, query, _ = logits.shape
+    slot = PAD
+    dma = pltpu.SemaphoreType.DMA
+    return pl.pallas_call(
+        functools.partial(forward_kernel, dims),
+        out_shape=(
+            shape_of((depth, own), BF16),
+            shape_of((depth, own), BF16),
+            shape_of((depth, own), BF16),
+            shape_of((nwa, nta) + wp.shape, BF16),
+            shape_of((depth, seq), BF16),
+            shape_of((nta, width, seq), BF16),
+            shape_of((heads, query, seq), BF16),
+            shape_of((nta, width, query), F32),
+            shape_of((heads, nta * 8, query), F32),
+            shape_of((nta * 8, CHUNK), F32),
+            shape_of((depth, pcol.shape[1]), F32),
+            shape_of((8, prow.shape[1] * nwa), F32),
+        ),
+        in_specs=anywhere(3) + whole(4),
+        out_specs=tuple(whole(3) + anywhere(4) + whole(5)),
+        scratch_shapes=[
+            pltpu.VMEM((depth, seq), BF16),
+            pltpu.VMEM((width, nta * slot), BF16),
+            pltpu.VMEM((nta * slot, seq // nz), BF16),
+            pltpu.VMEM((depth, seq), BF16),
+            pltpu.VMEM((nta, width, seq), BF16),
+            pltpu.VMEM((heads, query, seq), BF16),
+            pltpu.VMEM((nta, width, query), BF16),
+            dma((2, 4, nz)),
+            dma((2, 2, nwa)),
+            dma((2, 2, nta)),
+            dma((2, 3, nz, nz)),
+            dma((2, 10, nz)),
+            dma((2, nwa, nz)),
+            dma((2, nta, max(nz, 2))),
+            dma((8,)),
+        ],
+        compiler_params=pltpu.CompilerParams(
+            collective_id=1, has_side_effects=True, vmem_limit_bytes=VMEM_BYTES
+        ),
+        cost_estimate=pl.CostEstimate(
+            flops=4 * 10**9, bytes_accessed=60 * 10**6, transcendentals=2 * 10**6
+        ),
+    )(tok, cot, wp, pcol, prow, ln, logits)
+
+
+def gelu_pair(u):
+    root = 0.7978845608028654
+    square = u * u
+    bent = jnp.tanh(root * u * (1.0 + 0.044715 * square))
+    low_half = 0.5 * (1.0 + bent)
+    slope = low_half + 0.5 * u * (1.0 - bent * bent) * root * (1.0 + 3.0 * 0.044715 * square)
+    return (u * low_half, slope)
+
+
+def middle_kernel(
+    dims,
+    attended,
+    xown,
+    cown,
+    pfull,
+    rfull,
+    ln,
+    block,
+    wo,
+    out,
+    dattended,
+    dresid,
+    gblock,
+    gwo,
+    vcol,
+    vrow,
+    resid,
+    normed,
+    inverse,
+    layer,
+    layer_t,
+    grad_t,
+    feed,
+    dlayer,
+    wide,
+):
+    nwa, nta = dims
+    step = pl.program_id(0)
+    wa = lax.axis_index("wa")
+    depth, own = xown.shape
+    width = depth // nwa
+    cols = block.shape[3] // 2
+    wdepth = depth // nta
+    up = block[:, 0, :, :cols].reshape(depth, cols)
+    down_t = block[:, 0, :, cols:].reshape(depth, cols)
+
+    def wide_wo():
+        joined = [
+            jnp.concatenate([wo[w, t] for t in range(nta)], axis=1) for w in range(nwa)
+        ]
+        return jnp.concatenate(joined, axis=0)
+
+    @pl.when(step == 0)
+    def _():
+        branch = lax.dot_general(wide_wo(), attended[...], ROWS_TN, preferred_element_type=F32)
+        branch = jnp.concatenate(
+            [branch[t * PAD : t * PAD + wdepth] for t in range(nta)], axis=0
+        )
+        res = xown[...].astype(F32) + branch + pfull[:, 3:4]
+        resid[...] = res
+        norm, inv = norm_stats(res)
+        normed[...] = norm
+        inverse[...] = jnp.broadcast_to(inv, inverse.shape)
+        low = (norm * pfull[:, 4:5] + pfull[:, 5:6]).astype(BF16)
+        layer[...] = low
+        layer_t[...] = low.T
+        grad_t[...] = cown[...].T
+        feed[...] = jnp.zeros_like(feed)
+        dlayer[...] = jnp.zeros_like(dlayer)
+
+    at = lanes(step * cols, cols)
+    upper = jnp.dot(layer_t[...], up, preferred_element_type=F32) + rfull[0:1, at]
+    hidden, slope = gelu_pair(upper)
+    hidden = hidden.astype(BF16)
+    dhidden = jnp.dot(grad_t[...], down_t, preferred_element_type=F32)
+    dupper = (dhidden * slope).astype(BF16)
+    vrow[:, at] = jnp.broadcast_to(
+        jnp.sum(dupper.astype(F32), axis=0, keepdims=True), (vrow.shape[0], cols)
+    )
+    feed[...] += lax.dot_general(down_t, hidden, ROWS_NT, preferred_element_type=F32)
+    dlayer[...] += lax.dot_general(up, dupper, ROWS_NT, preferred_element_type=F32)
+    gup = jnp.dot(layer[...], dupper, preferred_element_type=F32)
+    gdown = jnp.dot(cown[...], hidden, preferred_element_type=F32)
+    gblock[:, 0, :, :cols] = gup.reshape(nwa, width, cols).astype(BF16)
+    gblock[:, 0, :, cols:] = gdown.reshape(nwa, width, cols).astype(BF16)
+
+    @pl.when(step == pl.num_programs(0) - 1)
+    def _():
+        grad = cown[...].astype(F32)
+        out[...] = (resid[...] + feed[...] + pfull[:, 6:7]).astype(BF16)
+        dl = dlayer[...]
+        norm = normed[...]
+        e = dl * pfull[:, 4:5]
+        mean_e = jnp.sum(e, axis=0, keepdims=True) / depth
+        mean_n = jnp.sum(e * norm, axis=0, keepdims=True) / depth
+        dres = grad + inverse[0:1, :] * (e - mean_e - norm * mean_n)
+        dresid[...] = dres
+        low = dres.astype(BF16)
+        vcol[...] = jnp.zeros_like(vcol)
+        vcol[:, 3:4] = jnp.sum(low.astype(F32), axis=1, keepdims=True)
+        vcol[:, 4:5] = jnp.sum(dl * norm, axis=1, keepdims=True)
+        vcol[:, 5:6] = jnp.sum(dl, axis=1, keepdims=True)
+        vcol[:, 6:7] = jnp.sum(grad, axis=1, keepdims=True)
+        wide[...] = jnp.zeros_like(wide)
+        for t in range(nta):
+            wide[t * PAD : t * PAD + wdepth, :] = low[t * wdepth : (t + 1) * wdepth]
+        da = jnp.dot(wide_wo(), wide[...], preferred_element_type=F32)
+        lane = lax.broadcasted_iota(jnp.int32, (depth, own), 1)
+        place = (lane // CHUNK) * (CHUNK * nwa) + lane % CHUNK + wa * CHUNK
+        da = jnp.where(place.astype(F32) < ln[0:1, 0:1], da, 0.0)
+        dattended[...] = da.astype(BF16)
+        made = lax.dot_general(attended[...], wide[...], ROWS_NT, preferred_element_type=F32)
+        for t in range(nta):
+            gwo[:, t] = made[:, t * PAD : (t + 1) * PAD].reshape(nwa, width, PAD).astype(BF16)
+
+
+def run_middle(dims, attended, xown, cown, pfull, rfull, ln, weights):
+    nwa, nta = dims
+    depth, own = xown.shape
+    width = weights.shape[2]
+    both = weights.shape[3] - 2 * PAD
+    hidden = both // 2 * nta
+
+    def full(shape):
+        return pl.BlockSpec(shape, lambda i: (0,) * len(shape))
+
+    block = pl.BlockSpec((nwa, 1, width, both), lambda i: (0, i, 0, 0))
+    wo = pl.BlockSpec((nwa, nta, width, PAD), lambda i: (0, 0, 0, both // PAD))
+    return pl.pallas_call(
+        functools.partial(middle_kernel, dims),
+        grid=(nta,),
+        out_shape=(
+            shape_of((depth, own), BF16),
+            shape_of((depth, own), BF16),
+            shape_of((depth, own), F32),
+            shape_of((nwa, nta, width, both), BF16),
+            shape_of((nwa, nta, width, PAD), BF16),
+            shape_of((depth, PAD), F32),
+            shape_of((8, hidden), F32),
+        ),
+        in_specs=[
+            full((depth, own)),
+            full((depth, own)),
+            full((depth, own)),
+            full(pfull.shape),
+            full(rfull.shape),
+            full(ln.shape),
+            block,
+            wo,
+        ],
+        out_specs=(
+            full((depth, own)),
+            full((depth, own)),
+            full((depth, own)),
+            block,
+            full((nwa, nta, width, PAD)),
+            full((depth, PAD)),
+            full((8, hidden)),
+        ),
+        scratch_shapes=[
+            pltpu.VMEM((depth, own), F32),
+            pltpu.VMEM((depth, own), F32),
+            pltpu.VMEM((8, own), F32),
+            pltpu.VMEM((depth, own), BF16),
+            pltpu.VMEM((own, depth), BF16),
+            pltpu.VMEM((own, depth), BF16),
+            pltpu.VMEM((depth, own), F32),
+            pltpu.VMEM((depth, own), F32),
+            pltpu.VMEM((nta * PAD, own), BF16),
+        ],
+        compiler_params=pltpu.CompilerParams(vmem_limit_bytes=VMEM_BYTES),
+        cost_estimate=pl.CostEstimate(
+            flops=17 * 10**9, bytes_accessed=40 * 10**6, transcendentals=2 * 10**6
+        ),
+    )(attended, xown, cown, pfull, rfull, ln, weights, weights)
+
+
+def backward_kernel(
+    dims,
+    dattended,
+    outown,
+    dresid,
+    xown,
+    terms,
+    mixed,
+    zinv,
+    lens,
+    ln,
+    pfull,
+    layer,
+    weights,
+    vcol,
+    vrow,
+    scaled,
+    shift,
+    output,
+    tgrad,
+    vgrad,
+    vectors,
+    da,
+    partial,
+    paired,
+    up_in,
+    up_out,
+    down_in,
+    down_out,
+    dvalue,
+    dvown,
+    wv,
+    vsend,
+    vrecv,
+    tsend,
+    csend,
+    crecv,
+    csum,
+    crecv2,
+    sem_da,
+    sem_out,
+    sem_core,
+    sem_line,
+    sem_dv,
+    sem_tg,
+    sem_v,
+    sem_c,
+    sem_c2,
+    sem_local,
+):
+    nwa, nta = dims
+    me = Place(nwa, nta)
+    wa, ta, z, c = me.wa, me.ta, me.z, me.c
+    nz = me.nz
+    depth, own = dresid.shape
+    width = depth // nwa
+    wdepth = depth // nta
+    heads, query, seq = terms.shape
+    hdim = width // heads
+    part = seq // nz
+    me.enter()
+
+    def block_rows(w):
+        return rows_at(w * width, width, 32)
+
+    def da_copy(w, b, local):
+        core = wa // 2
+        src = dattended.at[block_rows(w), lanes(b * CHUNK)]
+        dst = da.at[ta, :, lanes((wa % 2) * CHUNK)]
+        if local:
+            return pltpu.make_async_copy(src, dst, sem_da.at[0, w, b])
+        return send(src, dst, sem_da.at[0, w, b], sem_da.at[1, ta, wa % 2], (w, 2 * b + core))
+
+    def da_self(w, b):
+        return jnp.logical_and(w == wa, 2 * b + wa // 2 == ta)
+
+    def da_start(k, carry):
+        w, b = (wa + k // nz) % nwa, k % nz
+
+        @pl.when(da_self(w, b))
+        def _():
+            da_copy(w, b, True).start()
+
+        @pl.when(jnp.logical_not(da_self(w, b)))
+        def _():
+            da_copy(w, b, False).start()
+
+        return carry
+
+    lax.fori_loop(0, nwa * nz, da_start, 0)
+
+    def back_copy(src, dst, sems, step, q):
+        w = (wa + step) % nwa
+        return send(
+            src.at[block_rows(w), pl.ds(q * CHUNK, CHUNK)],
+            dst.at[:, lanes(q * part + wa * CHUNK)],
+            sems.at[0, step, q],
+            sems.at[1, step, q],
+            (w, ta),
+        )
+
+    def back_own(src, dst, sems, q):
+        return pltpu.make_async_copy(
+            src.at[block_rows(wa), pl.ds(q * CHUNK, CHUNK)],
+            dst.at[:, lanes(q * part + wa * CHUNK)],
+            sems.at[0, 0, q],
+        )
+
+    for q in range(nz):
+        back_own(outown, output, sem_out, q).start()
+        for step in range(1, nwa):
+            back_copy(outown, output, sem_out, step, q).start()
+    get_wv = pltpu.make_async_copy(
+        weights.at[:, :, :, pl.ds(weights.shape[3] - PAD, PAD)], wv, sem_local.at[0]
+    )
+    get_wv.start()
+
+    def da_arrive(k, carry):
+        s, j = k // 2, k % 2
+        own_piece = jnp.logical_and(s == ta, 2 * c + j == wa)
+        where = da.at[s, :, lanes(j * CHUNK)]
+
+        @pl.when(jnp.logical_not(own_piece))
+        def _():
+            send(where, where, sem_da.at[0, 0, 0], sem_da.at[1, s, j], (2 * c + j, s)).wait_recv()
+
+        return carry
+
+    def da_sent(k, carry):
+        w, b = (wa + k // nz) % nwa, k % nz
+
+        @pl.when(da_self(w, b))
+        def _():
+            da_copy(w, b, True).wait()
+
+        @pl.when(jnp.logical_not(da_self(w, b)))
+        def _():
+            da_copy(w, b, False).wait_send()
+
+        return carry
+
+    lax.fori_loop(0, nwa * nz, da_sent, 0)
+    lax.fori_loop(0, 2 * nta, da_arrive, 0)
+
+    for h in range(heads):
+        group = slice(h * hdim, (h + 1) * hdim)
+        for s in range(nta):
+            one = da[s, group, :].astype(F32)
+            inv = zinv[h, s * 8 : s * 8 + 1, :]
+            along = jnp.sum(one * mixed[s, group, :], axis=0, keepdims=True)
+            shift[h, s * 8 : (s + 1) * 8, :] = jnp.broadcast_to(along * inv, (8, query))
+            scaled[s, group, :] = (one * inv).astype(BF16)
+    for h in range(heads):
+        group = slice(h * hdim, (h + 1) * hdim)
+        stacked = jnp.concatenate([scaled[s, group, :] for s in range(nta)], axis=0)
+        made = jnp.dot(stacked, terms[h], preferred_element_type=F32).astype(BF16)
+        for s in range(nta):
+            partial[s, group, :] = made[s * hdim : (s + 1) * hdim]
+
+    def core_copy(b, core):
+        return send(
+            partial.at[2 * b + core],
+            paired.at[b],
+            sem_core.at[0, b],
+            sem_core.at[1, b],
+            (wa, me.peer),
+        )
+
+    order = []
+    for j in range(nz):
+        for b in (nz - 1 - j, j):
+            if b not in order:
+                order.append(b)
+    for b in order:
+        core_copy(b, 1 - c).start()
+
+    def line_copy(up, j):
+        k = 0 if up else 1
+        return send(
+            (up_out if up else down_out).at[j],
+            (up_in if up else down_in).at[j],
+            sem_line.at[0, k, j],
+            sem_line.at[1, k, j],
+            (wa, ta + 2 if up else ta - 2),
+        )
+
+    ready = set()
+
+    def core_ready(b):
+        if b not in ready:
+            ready.add(b)
+            core_copy(b, c).wait_recv()
+
+    def chip_sum(b):
+        return partial[2 * b + c].astype(F32) + paired[b].astype(F32)
+
+    for j in range(nz - 1):
+        target = nz - 1 - j
+        core_ready(target)
+
+        @pl.when(z < target)
+        def _():
+            @pl.when(z > 0)
+            def _():
+                line_copy(True, j).wait_recv()
+                up_out[j] = (chip_sum(target) + up_in[j].astype(F32)).astype(BF16)
+
+            @pl.when(z == 0)
+            def _():
+                up_out[j] = chip_sum(target).astype(BF16)
+
+            line_copy(True, j).start()
+
+        core_ready(j)
+
+        @pl.when(z > j)
+        def _():
+            @pl.when(z < nz - 1)
+            def _():
+                line_copy(False, j).wait_recv()
+                down_out[j] = (chip_sum(j) + down_in[j].astype(F32)).astype(BF16)
+
+            @pl.when(z == nz - 1)
+            def _():
+                down_out[j] = chip_sum(j).astype(BF16)
+
+            line_copy(False, j).start()
+
+    for b in range(nz):
+        core_ready(b)
+    place = lax.broadcasted_iota(jnp.int32, (width, seq), 1).astype(F32)
+    key_valid = place < ln[0:1, 0:1]
+
+    @pl.when(z == 0)
+    def _():
+        line_copy(False, 0).wait_recv()
+        total = chip_sum(0) + down_in[0].astype(F32)
+        dvalue[...] = jnp.where(key_valid, total, 0.0).astype(BF16)
+
+    @pl.when(z == nz - 1)
+    def _():
+        line_copy(True, 0).wait_recv()
+        total = chip_sum(nz - 1) + up_in[0].astype(F32)
+        dvalue[...] = jnp.where(key_valid, total, 0.0).astype(BF16)
+
+    for b in range(1, nz - 1):
+
+        @pl.when(z == b)
+        def _():
+            line_copy(True, nz - 1 - b).wait_recv()
+            line_copy(False, b).wait_recv()
+            total = chip_sum(b) + up_in[nz - 1 - b].astype(F32) + down_in[b].astype(F32)
+            dvalue[...] = jnp.where(key_valid, total, 0.0).astype(BF16)
+
+    def dv_copy(step, q):
+        w = (wa + step) % nwa
+        return send(
+            dvalue.at[:, lanes(q * part + w * CHUNK)],
+            dvown.at[block_rows(wa), pl.ds(q * CHUNK, CHUNK)],
+            sem_dv.at[0, step, q],
+            sem_dv.at[1, step, q],
+            (w, ta),
+        )
+
+    for q in range(nz):
+        for step in range(1, nwa):
+            dv_copy(step, q).start()
+        dvown[block_rows(wa), q * CHUNK : (q + 1) * CHUNK] = dvalue[
+            :, lanes(q * part + wa * CHUNK)
+        ]
+
+    vmade = lax.dot_general(layer[...], dvalue[...], ROWS_NT, preferred_element_type=F32)
+    vsend[...] = vmade.astype(BF16).reshape(nta, wdepth, width)
+    vbias = jnp.sum(dvalue[...].astype(F32), axis=1, keepdims=True)
+
+    def v_copy(step):
+        t = (ta + step) % nta
+        return send(
+            vsend.at[t], vrecv.at[step], sem_v.at[0, step], sem_v.at[1, step], (wa, t)
+        )
+
+    for step in range(1, nta):
+        v_copy(step).start()
+
+    get_wv.wait()
+    for step in range(1, nwa):
+        for q in range(nz):
+            dv_copy(step, q).wait_recv()
+    dl_parts = []
+    for t in range(nta):
+        turned = jnp.concatenate([wv[w, t] for w in range(nwa)], axis=0)
+        dl_parts.append(
+            lax.dot_general(turned, dvown[...], ROWS_TN, preferred_element_type=F32)[:wdepth]
+        )
+    dl = jnp.concatenate(dl_parts, axis=0)
+    norm, inv = norm_stats(xown[...].astype(F32))
+    e = dl * pfull[:, 0:1]
+    mean_e = jnp.sum(e, axis=0, keepdims=True) / depth
+    mean_n = jnp.sum(e * norm, axis=0, keepdims=True) / depth
+    tsend[...] = (dresid[...] + inv * (e - mean_e - norm * mean_n)).astype(BF16)
+    for q in range(nz):
+        back_own(tsend, tgrad, sem_tg, q).start()
+        for step in range(1, nwa):
+            back_copy(tsend, tgrad, sem_tg, step, q).start()
+
+    gain = jnp.sum(dl * norm, axis=1, keepdims=True)
+    bias = jnp.sum(dl, axis=1, keepdims=True)
+    column = lax.broadcasted_iota(jnp.int32, (depth, PAD), 1)
+    cols = jnp.where(column == 0, gain, jnp.where(column == 1, bias, vcol[...]))
+    wide = vrow.shape[1] // nwa
+    gap = csend.shape[2] - wide
+    for w in range(nwa):
+        piece = cols[w * width : (w + 1) * width]
+        piece = jnp.concatenate([piece, jnp.zeros((gap - width, PAD), F32)], axis=0)
+        csend[w, :, :gap] = piece.T[:8]
+        csend[w, :, gap:] = vrow[:, w * wide : (w + 1) * wide]
+
+    def c_copy(step):
+        w = (wa + step) % nwa
+        return send(csend.at[w], crecv.at[step], sem_c.at[0, step], sem_c.at[1, step], (w, ta))
+
+    for step in range(1, nwa):
+        c_copy(step).start()
+    crecv[0] = csend[wa]
+    piece = jnp.concatenate(
+        [jnp.broadcast_to(vbias, (width, PAD)), jnp.zeros((gap - width, PAD), F32)], axis=0
+    )
+    vb_row = jnp.concatenate([piece.T[:8], jnp.zeros((8, wide), F32)], axis=1)
+    row = lax.broadcasted_iota(jnp.int32, vb_row.shape, 0)
+    total = jnp.where(row == 2, vb_row, 0.0) + crecv[0]
+    for step in range(1, nwa):
+        c_copy(step).wait_recv()
+        total = total + crecv[step]
+    csum[...] = total
+
+    def c2_copy(step):
+        t = (ta + step) % nta
+        return send(csum, crecv2.at[step], sem_c2.at[0, step], sem_c2.at[1, step], (wa, t))
+
+    for step in range(1, nta):
+        c2_copy(step).start()
+    value_total = vsend[ta].astype(F32)
+    for step in range(1, nta):
+        v_copy(step).wait_recv()
+        value_total = value_total + vrecv[step].astype(F32)
+    vgrad[...] = value_total
+    crecv2[0] = csum[...]
+    for step in range(1, nta):
+        c2_copy(step).wait_recv()
+    full = jnp.zeros(csum.shape, F32)
+    for t in range(nta):
+        full = full + crecv2[(ta - t + nta) % nta]
+    vectors[...] = full
+
+    for step in range(1, nwa):
+        for q in range(nz):
+            back_copy(tsend, tgrad, sem_tg, step, q).wait()
+            back_copy(outown, output, sem_out, step, q).wait()
+            dv_copy(step, q).wait_send()
+        c_copy(step).wait_send()
+    for q in range(nz):
+        back_own(outown, output, sem_out, q).wait()
+        back_own(tsend, tgrad, sem_tg, q).wait()
+    for step in range(1, nta):
+        v_copy(step).wait_send()
+        c2_copy(step).wait_send()
+    for b in range(nz):
+        core_copy(b, 1 - c).wait_send()
+    for j in range(nz - 1):
+
+        @pl.when(z < nz - 1 - j)
+        def _():
+            line_copy(True, j).wait_send()
+
+        @pl.when(z > j)
+        def _():
+            line_copy(False, j).wait_send()
+
+
+def run_backward(
+    dims, dattended, outown, dresid, xown, terms, mixed, zinv, lens, ln, pfull, layer, weights, vcol, vrow
+):
+    nwa, nta = dims
+    nz = nta // 2
+    depth, own = dresid.shape
+    width = depth // nwa
+    heads, query, seq = terms.shape
+    wdepth = depth // nta
+    wide = 256 + vrow.shape[1] // nwa
+    dma = pltpu.SemaphoreType.DMA
+    return pl.pallas_call(
+        functools.partial(backward_kernel, dims),
+        out_shape=(
+            shape_of((nta, width, query), BF16),
+            shape_of((heads, nta * 8, query), F32),
+            shape_of((width, seq), BF16),
+            shape_of((width, seq), BF16),
+            shape_of((wdepth, width), F32),
+            shape_of((8, wide), F32),
+        ),
+        in_specs=whole(11) + anywhere(1) + whole(2),
+        out_specs=tuple(whole(6)),
+        scratch_shapes=[
+            pltpu.VMEM((nta, width, query), BF16),
+            pltpu.VMEM((nta, width, seq), BF16),
+            pltpu.VMEM((nz, width, seq), BF16),
+            pltpu.VMEM((nz - 1, width, seq), BF16),
+            pltpu.VMEM((nz - 1, width, seq), BF16),
+            pltpu.VMEM((nz - 1, width, seq), BF16),
+            pltpu.VMEM((nz - 1, width, seq), BF16),
+            pltpu.VMEM((width, seq), BF16),
+            pltpu.VMEM((depth, own), BF16),
+            pltpu.VMEM((nwa, nta, width, PAD), BF16),
+            pltpu.VMEM((nta, wdepth, width), BF16),
+            pltpu.VMEM((nta, wdepth, width), BF16),
+            pltpu.VMEM((depth, own), BF16),
+            pltpu.VMEM((nwa, 8, wide), F32),
+            pltpu.VMEM((nwa, 8, wide), F32),
+            pltpu.VMEM((8, wide), F32),
+            pltpu.VMEM((nta, 8, wide), F32),
+            dma((2, nta, max(nz, 2))),
+            dma((2, nwa, nz)),
+            dma((2, nz)),
+            dma((2, 2, nz)),
+            dma((2, nwa, nz)),
+            dma((2, nwa, nz)),
+            dma((2, nta)),
+            dma((2, nwa)),
+            dma((2, nta)),
+            dma((2,)),
+        ],
+        compiler_params=pltpu.CompilerParams(
+            collective_id=2, has_side_effects=True, vmem_limit_bytes=VMEM_BYTES
+        ),
+        cost_estimate=pl.CostEstimate(
+            flops=4 * 10**9, bytes_accessed=80 * 10**6, transcendentals=0
+        ),
+    )(dattended, outown, dresid, xown, terms, mixed, zinv, lens, ln, pfull, layer, weights, vcol, vrow)
+
+
+def logits_kernel(terms, scaled, value, shift, lens, out):
+    nta = scaled.shape[0]
+    cols = terms.shape[2]
+    stacked = jnp.concatenate([scaled[s] for s in range(nta)], axis=0)
+    values = jnp.concatenate([value[s] for s in range(nta)], axis=0)
+    made = lax.dot_general(stacked, values, ROWS_TN, preferred_element_type=F32)
+    where = (nta * 8, cols)
+    place = lax.broadcasted_iota(jnp.int32, where, 1) + pl.program_id(1) * cols
+    first = lax.broadcasted_iota(jnp.int32, where, 0) % 8 == 0
+    valid = jnp.logical_and(place.astype(F32) < lens[:, 0:1], first)
+    valid = jnp.where(valid, 1.0, 0.0).astype(BF16)
+    high = shift[0].astype(BF16)
+    rest = (shift[0] - high.astype(F32)).astype(BF16)
+    made = made - lax.dot_general(high, valid, ROWS_TN, preferred_element_type=F32)
+    made = made - lax.dot_general(rest, valid, ROWS_TN, preferred_element_type=F32)
+    out[0] = terms[0].astype(F32) * made
+
+
+def run_logits(terms, scaled, value, shift, lens):
+    heads, query, seq = terms.shape
+    nta, width, _ = scaled.shape
+    hdim = width // heads
+    cols = min(1024, seq)
+    return pl.pallas_call(
+        logits_kernel,
+        grid=(heads, seq // cols),
+        out_shape=shape_of((heads, query, seq), F32),
+        in_specs=[
+            pl.BlockSpec((1, query, cols), lambda h, k: (h, 0, k)),
+            pl.BlockSpec((nta, hdim, query), lambda h, k: (0, h, 0)),
+            pl.BlockSpec((nta, hdim, cols), lambda h, k: (0, h, k)),
+            pl.BlockSpec((1, nta * 8, query), lambda h, k: (h, 0, 0)),
+            pl.BlockSpec(lens.shape, lambda h, k: (0, 0)),
+        ],
+        out_specs=pl.BlockSpec((1, query, cols), lambda h, k: (h, 0, k)),
+        compiler_params=pltpu.CompilerParams(vmem_limit_bytes=VMEM_BYTES),
+        cost_estimate=pl.CostEstimate(
+            flops=2 * 10**9, bytes_accessed=16 * 10**6, transcendentals=0
+        ),
+    )(terms, scaled, value, shift, lens)
+
+
+def on_device_fast(
+    dims,
+    tokens,
+    seq_lengths,
+    norm1_gain,
+    norm1_bias,
+    value_weight,
+    value_bias,
+    synth_logits,
+    out_weight,
+    out_bias,
+    norm2_gain,
+    norm2_bias,
+    up_weight,
+    up_bias,
+    down_weight,
+    down_bias,
+    cotangent,
+):
+    nwa, nta = dims
+    width = tokens.shape[0]
+    slim = ((0, 0), (0, PAD - out_weight.shape[1]))
+    packed = jnp.concatenate(
+        [up_weight, down_weight.T, jnp.pad(out_weight, slim), jnp.pad(value_weight.T, slim)], axis=1
+    )
+    per_feature = (
+        norm1_gain,
+        norm1_bias,
+        value_bias,
+        out_bias,
+        norm2_gain,
+        norm2_bias,
+        down_bias,
+    )
+    pcol = jnp.pad(jnp.stack(per_feature, axis=1), ((0, 0), (0, PAD - len(per_feature))))
+    prow = jnp.broadcast_to(up_bias[None, :], (8, up_bias.shape[0]))
+    ln = jnp.broadcast_to(seq_lengths.astype(F32)[:, None], (8, CHUNK))
+    logits = synth_logits.transpose(1, 0, 2)
+    (
+        xown,
+        cown,
+        attended,
+        weights,
+        layer,
+        value,
+        terms,
+        mixed,
+        zinv,
+        lens,
+        pfull,
+        rfull,
+    ) = run_forward(dims, tokens, cotangent, packed, pcol, prow, ln, logits)
+    outown, dattended, dresid, gblock, gwo, vcol, vrow = run_middle(
+        dims, attended, xown, cown, pfull, rfull, ln, weights
+    )
+    both = gblock.shape[3]
+    gblock = lax.psum_scatter(
+        gblock.reshape(-1, both), ("wa", "ta"), scatter_dimension=0, tiled=True
+    )
+    gwo = lax.psum_scatter(gwo.reshape(-1, PAD), ("wa", "ta"), scatter_dimension=0, tiled=True)
+    scaled, shift, output, tgrad, vgrad, vectors = run_backward(
+        dims,
+        dattended,
+        outown,
+        dresid,
+        xown,
+        terms,
+        mixed,
+        zinv,
+        lens,
+        ln,
+        pfull,
+        layer,
+        weights,
+        vcol,
+        vrow,
+    )
+    logits_grad = run_logits(terms, scaled, value, shift, lens)
+    cols = both // 2
+    gap = vectors.shape[1] - up_bias.shape[0]
+    return (
+        output,
+        tgrad.astype(F32),
+        vectors[0, :width],
+        vectors[1, :width],
+        vgrad,
+        vectors[2, :width],
+        logits_grad.transpose(1, 0, 2),
+        gwo[:, : out_weight.shape[1]].astype(F32),
+        vectors[3, :width],
+        vectors[4, :width],
+        vectors[5, :width],
+        gblock[:, :cols].astype(F32),
+        vectors[0, gap:],
+        gblock[:, cols:].T.astype(F32),
+        vectors[6, :width],
+    )
+
+
+def fits(mesh):
+    return mesh.shape["wa"] == 4 and mesh.shape["ta"] == 8
+
+
 def solution(mesh):
     placed = (
         P("wa", "ta"),
@@ -242,8 +1588,10 @@
         P("wa"),
         P("wa", "ta"),
     )
+    sizes = (mesh.shape["wa"], mesh.shape["ta"])
+    body = functools.partial(on_device_fast, sizes) if fits(mesh) else on_device
     return jax.shard_map(
-        on_device,
+        body,
         mesh=mesh,
         in_specs=placed,
         out_specs=(

time: 1020 us -> 444 us (0.44)
  waiting for transfers between devices: 562 us -> 84.6 us
  Pallas kernels: 0 us -> 328 us
  blocking collectives: 251 us -> 0 us
  matrix products: 88.5 us -> 0 us
  local copies, waits for them, and re-layouts: 55.8 us -> 8.78 us
  other arithmetic: 29 us -> 7.59 us
  starting transfers between devices: 13.7 us -> 0.08 us
    pallas_call x0 -> x4, Pallas kernels: none -> 328 us  [the longest x1 145 us: run_forward(): pl.pallas_call(functools.partial(forward_kernel, dims), out_shape=(shape_...]
    reduce_scatter x8 -> x2, waiting for transfers between devices: 334 us -> 83.8 us  [the longest x1 83.8 us: on_device_fast(): lax.psum_scatter(gblock.reshape(-1, both), ('wa', 'ta'), scatter_dimensio...]
    all_gather x7 -> x0, waiting for transfers between devices: 226 us -> none  [the longest x4 156 us: all_features(): return lax.all_gather(features_part, 'wa', axis=1, tiled=True)]
    all_to_all x3 -> x0, blocking collectives: 107 us -> none  [the longest x1 44.3 us: on_device(): lax.all_to_all(up_part, 'wa', split_axis=1, concat_axis=0, tiled=True)]
    psum x5 -> x0, blocking collectives: 93 us -> none  [the longest x4 64.2 us: row_statistics(): lax.psum((jnp.sum(first_term, axis=1), jnp.sum(second_term, axis=1)), 'wa')]
    dot_general x17 -> x0, matrix products: 84.4 us -> none  [the longest x1 11.5 us: on_device(): lax.dot_general(grad_full, down_block, ALONG_FEATURES, preferred_element_...]
    all_gather x2 -> x0, blocking collectives: 42.8 us -> none  [the longest x1 27.9 us: on_device(): lax.all_gather(out_weight, 'ta', axis=1, tiled=True)]
    unnamed x92 -> x7, local copies, waits for them, and re-layouts: 34.8 us -> 2.43 us
  transfers between devices with their start and end apart: 19 -> 2, of which waited for: 14 -> 1; matrix products, arithmetic and copies ran while one was open for 9% -> 2% of each run, Pallas kernels for 0% -> 34%
where the time goes in v2:
time: 444 us
  Pallas kernels  328 us (74%)
  waiting for transfers between devices  84.6 us (19%)
  between operations  14.7 us (3%)
  local copies, waits for them, and re-layouts  8.78 us (2%)
  other arithmetic  7.59 us (2%)
    pallas_call x1, Pallas kernels, run_forward(): pl.pallas_call(functools.partial(forward_kernel, dims), out_shape=(shape_...  145 us
    pallas_call x1, Pallas kernels, run_backward(): pl.pallas_call(functools.partial(backward_kernel, dims), out_shape=(shape...  139 us
    reduce_scatter x1, waiting for transfers between devices, on_device_fast(): lax.psum_scatter(gblock.reshape(-1, both), ('wa', 'ta'), scatter_dimensio...  83.8 us
    pallas_call x1, Pallas kernels, run_middle(): pl.pallas_call(functools.partial(middle_kernel, dims), grid=(nta,), out_s...  33.4 us
    pallas_call x1, Pallas kernels, run_logits(): pl.pallas_call(logits_kernel, grid=(heads, seq // cols), out_shape=shape_...  10.1 us
  transfers between devices with their start and end apart: 2, of which 1 were waited for; matrix products, arithmetic and copies ran while one was open for 2% of the time, Pallas kernels for 34%

profile of v2, /device:TPU:0, one launch (start us, length us, event | category | flops | bytes accessed | tf_op | source)
XLA Modules:
  0.0 443.8 jit_solution(7495520097433688033)
XLA Ops:
  7.2 0.0 reduce-scatter.3.cloned.1.call-start
  7.9 0.9 copy.40
  8.8 0.8 stack.31
  9.6 0.1 copy.41
  9.7 0.7 pad.13.pcol
  10.4 1.8 fusion.4.wp
  12.2 0.6 broadcast_in_dim.16.ln
  12.8 1.3 broadcast_in_dim.6.prow
  14.1 145.3 %shard_map.271 = (bf16[768,512]{1,0:T(8,128)(2,1)}, bf16[768,512]{1,0:T(8,128)(2,1)}, bf16[768,512]{1,0:T(8,128)(2,1)}, bf16[4,8,192,1024]{3,2,1,0:T(8,128)(2,1)...) custom-call(bf16[192,2048]{1,0:T(8,128)(2,1)} %tok.1, ...), custom_call_target="tpu_custom_call" | custom-call | flops 4000000000 | bytes 60000000 | tf_op jit(solution)/shard_map/pallas_call | solution.py:766
  159.4 33.4 %shard_map.272 = (bf16[768,512]{1,0:T(8,128)(2,1)}, bf16[768,512]{1,0:T(8,128)(2,1)}, f32[768,512]{1,0:T(8,128)}, bf16[4,8,192,768]{3,2,1,0:T(8,128)(2,1)}, bf16...) custom-call(bf16[768,512]{1,0:T(8,128)(2,1)} %get-tuple-element.40.attended, ...), custom_call_target="tpu_custom_call" | custom-call | flops 16999999488 | bytes 40000000 | tf_op jit(solution)/shard_map/pallas_call | solution.py:938
  192.8 0.0 reduce-scatter.3.cloned.1.call-update
  192.8 0.0 reduce-scatter.5.cloned.1.call-start
  192.9 0.7 reduce-scatter.5.cloned.1.call-update
  193.6 139.2 %shard_map.273 = (bf16[8,192,256]{2,1,0:T(8,128)(2,1)}, f32[3,64,256]{2,1,0:T(8,128)}, bf16[192,2048]{1,0:T(8,128)(2,1)}, bf16[192,2048]{1,0:T(8,128)(2,1)}, f32[96,192]{1,0:T(8,128)}, /*index=5*/f32[8,1024]{1,0:T(8,128)}) custom-call(bf16[768,512]{1,0:T(8,128)(2,1)} %get-tuple-element.46.dattended, bf16[768,512]{1,0:T(8,128)(2,1)} %get-tuple-element.47.outown, ...), custom_call_target="tpu_custom_call" | custom-call | flops 4000000000 | bytes 80000000 | tf_op jit(solution)/shard_map/pallas_call | solution.py:1377
  332.8 2.5 convert_element_type.24
  335.3 1.3 slice_reduce_fusion
  336.7 0.0 copy-start
  336.7 0.0 copy-start.1
  336.7 10.1 %shard_map.274 = f32[3,256,2048]{2,1,0:T(8,128)} custom-call(bf16[3,256,2048]{2,1,0:T(8,128)(2,1)} %get-tuple-element.49.terms, bf16[8,192,256]{2,1,0:T(8,128)(2,1)} %get-tuple-element.60.scaled, bf16[8,192,2048]{2,1,0:T(8,128)(2,1)} %get-tuple-element.61.value, f32[3,64,256]{2,1,0:T(8,128)} %get-tuple-element.62.shift, f32[64,128]{1,0:T(8,128)} %get-tuple-element.52.lens), custom_call_target="tpu_custom_call" | custom-call | flops 2000000000 | bytes 16000000 | tf_op jit(solution)/shard_map/pallas_call | solution.py:1450
  346.8 1.5 fusion.5
  348.3 0.0 reduce-scatter.3.cloned.1.call-done
  348.4 1.4 slice_convert_fusion.1
  349.8 83.8 %reduce-scatter.5.cloned.1.call-done = bf16[192,768]{1,0:T(8,128)(2,1)} async-done(((bf16[6144,768]{1,0:T(8,128)(2,1)}), bf16[192,768]{1,0:T(8,128)(2,1)}) %reduce-scatter.5.cloned.1.call-update) | async-done | bytes 294928 | tf_op jit(solution)/shard_map/reduce_scatter | solution.py:1525
  433.6 1.8 convert_bitcast_fusion
  435.5 0.0 copy-done
  435.5 0.9 copy.45
  436.4 0.0 copy-done.1
  436.4 0.6 copy.46
Async XLA Ops:
  7.2 341.2 %reduce-scatter.3.cloned.1.call-start = ((), (), s32[]{:S(2)}) async-start(), calls=%async_computation.2 | async-start | bytes 1622016 | tf_op jit(solution)/shard_map/reduce_scatter | solution.py:1528
  192.8 240.8 %reduce-scatter.5.cloned.1.call-start = ((), (), s32[]{:S(2)}) async-start(), calls=%async_computation.3 | async-start | bytes 9732096 | tf_op jit(solution)/shard_map/reduce_scatter | solution.py:1525
  336.7 98.8 %copy-start = (bf16[192,2048]{1,0:T(8,128)(2,1)S(1)}, bf16[192,2048]{1,0:T(8,128)(2,1)}, u32[]{:S(2)}) copy-start(bf16[192,2048]{1,0:T(8,128)(2,1)} %get-tuple-element.89) | copy-start | bytes 2359300
  336.7 99.7 %copy-start.1 = (f32[96,192]{1,0:T(8,128)S(1)}, f32[96,192]{1,0:T(8,128)}, u32[]{:S(2)}) copy-start(f32[96,192]{1,0:T(8,128)} %get-tuple-element.93) | copy-start | bytes 221188
Sparse Core Ops, SparseCore 0:
  192.9 99.2 reduce-scatter.2
  298.2 135.4 reduce-scatter.4

commit v3 on v2

--- a/solution.py
+++ b/solution.py
@@ -829,8 +829,7 @@
     out,
     dattended,
     dresid,
-    gblock,
-    gwo,
+    wgrad,
     vcol,
     vrow,
     resid,
@@ -842,9 +841,13 @@
     feed,
     dlayer,
     wide,
+    gblock,
+    gwo,
+    sem_g,
 ):
     nwa, nta = dims
     step = pl.program_id(0)
+    last = pl.num_programs(0) - 1
     wa = lax.axis_index("wa")
     depth, own = xown.shape
     width = depth // nwa
@@ -890,10 +893,27 @@
     dlayer[...] += lax.dot_general(up, dupper, ROWS_NT, preferred_element_type=F32)
     gup = jnp.dot(layer[...], dupper, preferred_element_type=F32)
     gdown = jnp.dot(cown[...], hidden, preferred_element_type=F32)
-    gblock[:, 0, :, :cols] = gup.reshape(nwa, width, cols).astype(BF16)
-    gblock[:, 0, :, cols:] = gdown.reshape(nwa, width, cols).astype(BF16)
-
-    @pl.when(step == pl.num_programs(0) - 1)
+
+    def put(at_step, slot):
+        return pltpu.make_async_copy(
+            gblock.at[slot],
+            wgrad.at[:, at_step // 2, at_step % 2, :, pl.ds(0, 2 * cols)],
+            sem_g.at[slot],
+        )
+
+    for slot in range(2):
+
+        @pl.when(step % 2 == slot)
+        def _():
+            @pl.when(step >= 2)
+            def _():
+                put(step - 2, slot).wait()
+
+            gblock[slot, :, :, :cols] = gup.reshape(nwa, width, cols).astype(BF16)
+            gblock[slot, :, :, cols:] = gdown.reshape(nwa, width, cols).astype(BF16)
+            put(step, slot).start()
+
+    @pl.when(step == last)
     def _():
         grad = cown[...].astype(F32)
         out[...] = (resid[...] + feed[...] + pfull[:, 6:7]).astype(BF16)
@@ -920,7 +940,15 @@
         dattended[...] = da.astype(BF16)
         made = lax.dot_general(attended[...], wide[...], ROWS_NT, preferred_element_type=F32)
         for t in range(nta):
-            gwo[:, t] = made[:, t * PAD : (t + 1) * PAD].reshape(nwa, width, PAD).astype(BF16)
+            piece = made[:, t * PAD : (t + 1) * PAD].reshape(nwa, width, PAD)
+            gwo[:, t // 2, t % 2] = piece.astype(BF16)
+        rest = pltpu.make_async_copy(
+            gwo, wgrad.at[:, :, :, :, pl.ds(2 * cols, PAD)], sem_g.at[2]
+        )
+        rest.start()
+        put(last - 1, (nta - 2) % 2).wait()
+        put(last, (nta - 1) % 2).wait()
+        rest.wait()
 
 
 def run_middle(dims, attended, xown, cown, pfull, rfull, ln, weights):
@@ -942,8 +970,7 @@
             shape_of((depth, own), BF16),
             shape_of((depth, own), BF16),
             shape_of((depth, own), F32),
-            shape_of((nwa, nta, width, both), BF16),
-            shape_of((nwa, nta, width, PAD), BF16),
+            shape_of((nwa, nta // 2, 2, width, both + PAD), BF16),
             shape_of((depth, PAD), F32),
             shape_of((8, hidden), F32),
         ),
@@ -961,8 +988,7 @@
             full((depth, own)),
             full((depth, own)),
             full((depth, own)),
-            block,
-            full((nwa, nta, width, PAD)),
+            pl.BlockSpec(memory_space=pl.ANY),
             full((depth, PAD)),
             full((8, hidden)),
         ),
@@ -976,6 +1002,9 @@
             pltpu.VMEM((depth, own), F32),
             pltpu.VMEM((depth, own), F32),
             pltpu.VMEM((nta * PAD, own), BF16),
+            pltpu.VMEM((2, nwa, width, both), BF16),
+            pltpu.VMEM((nwa, nta // 2, 2, width, PAD), BF16),
+            pltpu.SemaphoreType.DMA((3,)),
         ],
         compiler_params=pltpu.CompilerParams(vmem_limit_bytes=VMEM_BYTES),
         cost_estimate=pl.CostEstimate(
@@ -998,6 +1027,7 @@
     pfull,
     layer,
     weights,
+    wgrad,
     vcol,
     vrow,
     scaled,
@@ -1006,13 +1036,20 @@
     tgrad,
     vgrad,
     vectors,
+    wsum,
     da,
     partial,
     paired,
     up_in,
-    up_out,
     down_in,
-    down_out,
+    gown,
+    gpeer,
+    first_x,
+    first_y,
+    second_x,
+    second_y,
+    gup_in,
+    gdown_in,
     dvalue,
     dvown,
     wv,
@@ -1033,6 +1070,8 @@
     sem_c,
     sem_c2,
     sem_local,
+    sem_g,
+    sem_gline,
 ):
     nwa, nta = dims
     me = Place(nwa, nta)
@@ -1100,6 +1139,136 @@
         weights.at[:, :, :, pl.ds(weights.shape[3] - PAD, PAD)], wv, sem_local.at[0]
     )
     get_wv.start()
+
+    half = width // 2
+    order = []
+    for j in range(nz):
+        for b in (nz - 1 - j, j):
+            if b not in order:
+                order.append(b)
+
+    def g_core(b, core):
+        return send(
+            wgrad.at[:, b, core],
+            gpeer.at[b],
+            sem_g.at[0, 0, b],
+            sem_g.at[1, 0, b],
+            (wa, me.peer),
+        )
+
+    def g_load(b):
+        return pltpu.make_async_copy(wgrad.at[:, b, c], gown.at[b], sem_g.at[0, 7, b])
+
+    def g_first(k, r, b):
+        near = me.wx if k == 0 else me.wy
+        which = near if r == 0 else me.wd
+        return send(
+            gown.at[b, which, pl.ds(k * half, half)],
+            (first_x if k == 0 else first_y).at[b, r],
+            sem_g.at[0, 1 + 2 * k + r, b],
+            sem_g.at[1, 1 + 2 * k + r, b],
+            (near, ta),
+        )
+
+    def g_second(k, b):
+        near = me.wy if k == 0 else me.wx
+        return send(
+            gown.at[b, near, pl.ds(k * half, half)],
+            (second_x if k == 0 else second_y).at[b],
+            sem_g.at[0, 5 + k, b],
+            sem_g.at[1, 5 + k, b],
+            (near, ta),
+        )
+
+    def g_add(b, which, k, extra):
+        rows = pl.ds(k * half, half)
+        gown[b, which, rows, :] = (
+            gown[b, which, rows, :].astype(F32) + extra.astype(F32)
+        ).astype(BF16)
+
+    def g_cores(b):
+        g_load(b).wait()
+        g_core(b, c).wait_recv()
+        for w in range(nwa):
+            gown[b, w] = (gown[b, w].astype(F32) + gpeer[b, w].astype(F32)).astype(BF16)
+        for k in range(2):
+            for r in range(2):
+                g_first(k, r, b).start()
+
+    def g_plane(b):
+        for k in range(2):
+            for r in range(2):
+                g_first(k, r, b).wait_recv()
+            landed = first_x if k == 0 else first_y
+            g_add(b, me.wy if k == 0 else me.wx, k, landed[b, 1])
+            g_second(k, b).start()
+            g_add(b, wa, k, landed[b, 0])
+
+    def g_end(b):
+        for k in range(2):
+            g_second(k, b).wait_recv()
+            g_add(b, wa, k, (second_x if k == 0 else second_y)[b])
+
+    def g_line(up, j):
+        k = 0 if up else 1
+        target = nz - 1 - j if up else j
+        return send(
+            gown.at[target, wa],
+            (gup_in if up else gdown_in).at[j],
+            sem_gline.at[0, k, j],
+            sem_gline.at[1, k, j],
+            (wa, ta + 2 if up else ta - 2),
+        )
+
+    def g_hop(j):
+        target = nz - 1 - j
+
+        @pl.when(z < target)
+        def _():
+            @pl.when(z > 0)
+            def _():
+                g_line(True, j).wait_recv()
+                gown[target, wa] = (
+                    gown[target, wa].astype(F32) + gup_in[j].astype(F32)
+                ).astype(BF16)
+
+            g_line(True, j).start()
+
+        @pl.when(z > j)
+        def _():
+            @pl.when(z < nz - 1)
+            def _():
+                g_line(False, j).wait_recv()
+                gown[j, wa] = (gown[j, wa].astype(F32) + gdown_in[j].astype(F32)).astype(BF16)
+
+            g_line(False, j).start()
+
+    def g_final():
+        @pl.when(z == 0)
+        def _():
+            g_line(False, 0).wait_recv()
+            wsum[...] = gown[0, wa].astype(F32) + gdown_in[0].astype(F32)
+
+        @pl.when(z == nz - 1)
+        def _():
+            g_line(True, 0).wait_recv()
+            wsum[...] = gown[nz - 1, wa].astype(F32) + gup_in[0].astype(F32)
+
+        for b in range(1, nz - 1):
+
+            @pl.when(z == b)
+            def _():
+                g_line(True, nz - 1 - b).wait_recv()
+                g_line(False, b).wait_recv()
+                both = gup_in[nz - 1 - b].astype(F32) + gdown_in[b].astype(F32)
+                wsum[...] = gown[b, wa].astype(F32) + both
+
+    for b in order:
+        g_core(b, 1 - c).start()
+        g_load(b).start()
+
+    for b in order:
+        g_cores(b)
 
     def da_arrive(k, carry):
         s, j = k // 2, k % 2
@@ -1152,18 +1321,13 @@
             (wa, me.peer),
         )
 
-    order = []
-    for j in range(nz):
-        for b in (nz - 1 - j, j):
-            if b not in order:
-                order.append(b)
     for b in order:
         core_copy(b, 1 - c).start()
 
     def line_copy(up, j):
         k = 0 if up else 1
         return send(
-            (up_out if up else down_out).at[j],
+            partial.at[2 * (nz - 1 - j if up else j) + c],
             (up_in if up else down_in).at[j],
             sem_line.at[0, k, j],
             sem_line.at[1, k, j],
@@ -1189,11 +1353,11 @@
             @pl.when(z > 0)
             def _():
                 line_copy(True, j).wait_recv()
-                up_out[j] = (chip_sum(target) + up_in[j].astype(F32)).astype(BF16)
+                partial[2 * target + c] = (chip_sum(target) + up_in[j].astype(F32)).astype(BF16)
 
             @pl.when(z == 0)
             def _():
-                up_out[j] = chip_sum(target).astype(BF16)
+                partial[2 * target + c] = chip_sum(target).astype(BF16)
 
             line_copy(True, j).start()
 
@@ -1204,14 +1368,26 @@
             @pl.when(z < nz - 1)
             def _():
                 line_copy(False, j).wait_recv()
-                down_out[j] = (chip_sum(j) + down_in[j].astype(F32)).astype(BF16)
+                partial[2 * j + c] = (chip_sum(j) + down_in[j].astype(F32)).astype(BF16)
 
             @pl.when(z == nz - 1)
             def _():
-                down_out[j] = chip_sum(j).astype(BF16)
+                partial[2 * j + c] = chip_sum(j).astype(BF16)
 
             line_copy(False, j).start()
 
+        if j == 0:
+            g_plane(order[0])
+            g_plane(order[1])
+        if j == 1:
+            for b in order[2:]:
+                g_plane(b)
+            g_end(order[0])
+            g_end(order[1])
+            g_hop(0)
+
+    for b in order[2:]:
+        g_end(b)
     for b in range(nz):
         core_ready(b)
     place = lax.broadcasted_iota(jnp.int32, (width, seq), 1).astype(F32)
@@ -1268,6 +1444,8 @@
     for step in range(1, nta):
         v_copy(step).start()
 
+    for j in range(1, nz - 1):
+        g_hop(j)
     get_wv.wait()
     for step in range(1, nwa):
         for q in range(nz):
@@ -1325,6 +1503,7 @@
 
     for step in range(1, nta):
         c2_copy(step).start()
+    g_final()
     value_total = vsend[ta].astype(F32)
     for step in range(1, nta):
         v_copy(step).wait_recv()
@@ -1352,22 +1531,30 @@
         c2_copy(step).wait_send()
     for b in range(nz):
         core_copy(b, 1 - c).wait_send()
+        g_core(b, 1 - c).wait_send()
+        for k in range(2):
+            g_first(k, 0, b).wait_send()
+            g_first(k, 1, b).wait_send()
+            g_second(k, b).wait_send()
     for j in range(nz - 1):
 
         @pl.when(z < nz - 1 - j)
         def _():
             line_copy(True, j).wait_send()
+            g_line(True, j).wait_send()
 
         @pl.when(z > j)
         def _():
             line_copy(False, j).wait_send()
+            g_line(False, j).wait_send()
 
 
 def run_backward(
-    dims, dattended, outown, dresid, xown, terms, mixed, zinv, lens, ln, pfull, layer, weights, vcol, vrow
+    dims, dattended, outown, dresid, xown, terms, mixed, zinv, lens, ln, pfull, layer, weights, wgrad, vcol, vrow
 ):
     nwa, nta = dims
     nz = nta // 2
+    half, both = weights.shape[2] // 2, wgrad.shape[4]
     depth, own = dresid.shape
     width = depth // nwa
     heads, query, seq = terms.shape
@@ -1383,17 +1570,24 @@
             shape_of((width, seq), BF16),
             shape_of((wdepth, width), F32),
             shape_of((8, wide), F32),
+            shape_of((width, both), F32),
         ),
-        in_specs=whole(11) + anywhere(1) + whole(2),
-        out_specs=tuple(whole(6)),
+        in_specs=whole(11) + anywhere(2) + whole(2),
+        out_specs=tuple(whole(7)),
         scratch_shapes=[
             pltpu.VMEM((nta, width, query), BF16),
             pltpu.VMEM((nta, width, seq), BF16),
             pltpu.VMEM((nz, width, seq), BF16),
             pltpu.VMEM((nz - 1, width, seq), BF16),
             pltpu.VMEM((nz - 1, width, seq), BF16),
-            pltpu.VMEM((nz - 1, width, seq), BF16),
-            pltpu.VMEM((nz - 1, width, seq), BF16),
+            pltpu.VMEM((nz, nwa, width, both), BF16),
+            pltpu.VMEM((nz, nwa, width, both), BF16),
+            pltpu.VMEM((nz, 2, half, both), BF16),
+            pltpu.VMEM((nz, 2, half, both), BF16),
+            pltpu.VMEM((nz, half, both), BF16),
+            pltpu.VMEM((nz, half, both), BF16),
+            pltpu.VMEM((nz - 1, width, both), BF16),
+            pltpu.VMEM((nz - 1, width, both), BF16),
             pltpu.VMEM((width, seq), BF16),
             pltpu.VMEM((depth, own), BF16),
             pltpu.VMEM((nwa, nta, width, PAD), BF16),
@@ -1414,6 +1608,8 @@
             dma((2, nwa)),
             dma((2, nta)),
             dma((2,)),
+            dma((2, 8, nz)),
+            dma((2, 2, nz)),
         ],
         compiler_params=pltpu.CompilerParams(
             collective_id=2, has_side_effects=True, vmem_limit_bytes=VMEM_BYTES
@@ -1421,7 +1617,10 @@
         cost_estimate=pl.CostEstimate(
             flops=4 * 10**9, bytes_accessed=80 * 10**6, transcendentals=0
         ),
-    )(dattended, outown, dresid, xown, terms, mixed, zinv, lens, ln, pfull, layer, weights, vcol, vrow)
+    )(
+        dattended, outown, dresid, xown, terms, mixed, zinv, lens, ln, pfull, layer, weights, wgrad,
+        vcol, vrow,
+    )
 
 
 def logits_kernel(terms, scaled, value, shift, lens, out):
@@ -1518,15 +1717,10 @@
         pfull,
         rfull,
     ) = run_forward(dims, tokens, cotangent, packed, pcol, prow, ln, logits)
-    outown, dattended, dresid, gblock, gwo, vcol, vrow = run_middle(
+    outown, dattended, dresid, wgrad, vcol, vrow = run_middle(
         dims, attended, xown, cown, pfull, rfull, ln, weights
     )
-    both = gblock.shape[3]
-    gblock = lax.psum_scatter(
-        gblock.reshape(-1, both), ("wa", "ta"), scatter_dimension=0, tiled=True
-    )
-    gwo = lax.psum_scatter(gwo.reshape(-1, PAD), ("wa", "ta"), scatter_dimension=0, tiled=True)
-    scaled, shift, output, tgrad, vgrad, vectors = run_backward(
+    scaled, shift, output, tgrad, vgrad, vectors, wsum = run_backward(
         dims,
         dattended,
         outown,
@@ -1540,11 +1734,12 @@
         pfull,
         layer,
         weights,
+        wgrad,
         vcol,
         vrow,
     )
     logits_grad = run_logits(terms, scaled, value, shift, lens)
-    cols = both // 2
+    cols = up_weight.shape[1]
     gap = vectors.shape[1] - up_bias.shape[0]
     return (
         output,
@@ -1554,13 +1749,13 @@
         vgrad,
         vectors[2, :width],
         logits_grad.transpose(1, 0, 2),
-        gwo[:, : out_weight.shape[1]].astype(F32),
+        wsum[:, 2 * cols : 2 * cols + out_weight.shape[1]],
         vectors[3, :width],
         vectors[4, :width],
         vectors[5, :width],
-        gblock[:, :cols].astype(F32),
+        wsum[:, :cols],
         vectors[0, gap:],
-        gblock[:, cols:].T.astype(F32),
+        wsum[:, cols : 2 * cols].T,
         vectors[6, :width],
     )
 

time: 444 us -> 370 us (0.83); the launches traced: 444 us -> 365 us
  waiting for transfers between devices: 84.6 us -> 0 us
  Pallas kernels: 328 us -> 350 us
  between operations: 14.7 us -> 1.54 us
  other arithmetic: 7.59 us -> 3.12 us
    reduce_scatter x2 -> x0, waiting for transfers between devices: 83.8 us -> none  [the longest x1 83.8 us: on_device_fast(): lax.psum_scatter(gblock.reshape(-1, both), ('wa', 'ta'), scatter_dimensio...]
    pallas_call x1, Pallas kernels: 139 us -> 160 us  [run_backward(): pl.pallas_call(functools.partial(backward_kernel, dims), out_shape=(shape...]
  transfers between devices with their start and end apart: 2 -> 0, of which waited for: 1 -> 0; matrix products, arithmetic and copies ran while one was open for 2% -> 0% of each run, Pallas kernels for 34% -> 0%
where the time goes in v3:
time: 370 us; the launch traced here: 365 us
  Pallas kernels  350 us (95%)
  local copies, waits for them, and re-layouts  10.4 us (3%)
    pallas_call x1, Pallas kernels, run_backward(): pl.pallas_call(functools.partial(backward_kernel, dims), out_shape=(shape...  160 us
    pallas_call x1, Pallas kernels, run_forward(): pl.pallas_call(functools.partial(forward_kernel, dims), out_shape=(shape_...  145 us
    pallas_call x1, Pallas kernels, run_middle(): pl.pallas_call(functools.partial(middle_kernel, dims), grid=(nta,), out_s...  34.8 us
    pallas_call x1, Pallas kernels, run_logits(): pl.pallas_call(logits_kernel, grid=(heads, seq // cols), out_shape=shape_...  10 us

profile of v3, /device:TPU:0, one launch (start us, length us, event | category | flops | bytes accessed | tf_op | source)
XLA Modules:
  0.0 365.3 jit_solution(2992486233703281529)
XLA Ops:
  1.3 0.6 broadcast_in_dim.16.ln
  1.9 0.8 stack.31
  2.7 1.3 broadcast_in_dim.6.prow
  4.0 0.9 copy.40
  4.9 0.1 copy.41
  5.0 0.7 pad.13.pcol
  5.7 1.8 fusion.4.wp
  7.5 145.4 %shard_map.271 = (bf16[768,512]{1,0:T(8,128)(2,1)}, bf16[768,512]{1,0:T(8,128)(2,1)}, bf16[768,512]{1,0:T(8,128)(2,1)}, bf16[4,8,192,1024]{3,2,1,0:T(8,128)(2,1)...) custom-call(bf16[192,2048]{1,0:T(8,128)(2,1)} %tok.1, ...), custom_call_target="tpu_custom_call" | custom-call | flops 4000000000 | bytes 60000000 | tf_op jit(solution)/shard_map/pallas_call | solution.py:766
  152.8 34.8 %shard_map.272 = (bf16[768,512]{1,0:T(8,128)(2,1)}, bf16[768,512]{1,0:T(8,128)(2,1)}, f32[768,512]{1,0:T(8,128)}, bf16[4,4,2,192,896]{4,3,2,1,0:T(8,128)(2,1)}, f32[768,128]{1,0:T(8,128)}, /*index=5*/f32[8,3072]{1,0:T(8,128)}) custom-call(bf16[768,512]{1,0:T(8,128)(2,1)} %get-tuple-element.40.attended, bf16[768,512]{1,0:T(8,128)(2,1)} %get-tuple-element.41.xown, ...), custom_call_target="tpu_custom_call" | custom-call | flops 16999999488 | bytes 40000000 | tf_op jit(solution)/shard_map/pallas_call | solution.py:966
  187.7 160.1 %shard_map.273 = (bf16[8,192,256]{2,1,0:T(8,128)(2,1)}, f32[3,64,256]{2,1,0:T(8,128)}, bf16[192,2048]{1,0:T(8,128)(2,1)}, bf16[192,2048]{1,0:T(8,128)(2,1)}, f32...) custom-call(bf16[768,512]{1,0:T(8,128)(2,1)} %get-tuple-element.46.dattended, ...), custom_call_target="tpu_custom_call" | custom-call | flops 4000000000 | bytes 80000000 | tf_op jit(solution)/shard_map/pallas_call | solution.py:1564
  347.8 0.0 copy-start.2
  347.8 0.0 copy-start.1
  347.8 10.0 %shard_map.274 = f32[3,256,2048]{2,1,0:T(8,128)} custom-call(bf16[3,256,2048]{2,1,0:T(8,128)(2,1)} %get-tuple-element.49.terms, bf16[8,192,256]{2,1,0:T(8,128)(2,1)} %get-tuple-element.61.scaled, bf16[8,192,2048]{2,1,0:T(8,128)(2,1)} %get-tuple-element.62.value, f32[3,64,256]{2,1,0:T(8,128)} %get-tuple-element.63.shift, f32[64,128]{1,0:T(8,128)} %get-tuple-element.52.lens), custom_call_target="tpu_custom_call" | custom-call | flops 2000000000 | bytes 16000000 | tf_op jit(solution)/shard_map/pallas_call | solution.py:1649
  357.8 0.0 copy-start
  357.8 0.0 copy-start.3
  357.8 1.4 slice_reduce_fusion
  359.2 1.5 fusion.5
  360.8 0.0 copy-done.2
  360.8 0.6 slice.36
  361.4 0.8 slice_bitcast_fusion
  362.3 0.0 copy-done.1
  362.3 1.3 convert_element_type.12
  363.6 0.0 copy-done
  363.6 0.9 copy.45
  364.5 0.0 copy-done.3
  364.5 0.6 copy.46
Async XLA Ops:
  347.8 13.0 %copy-start.2 = (f32[192,896]{1,0:T(8,128)S(1)}, f32[192,896]{1,0:T(8,128)}, u32[]{:S(2)}) copy-start(f32[192,896]{1,0:T(8,128)} %get-tuple-element.64) | copy-start | bytes 2064388
  347.8 14.5 %copy-start.1 = (bf16[192,2048]{1,0:T(8,128)(2,1)S(1)}, bf16[192,2048]{1,0:T(8,128)(2,1)}, u32[]{:S(2)}) copy-start(bf16[192,2048]{1,0:T(8,128)(2,1)} %get-tuple-element.58) | copy-start | bytes 2359300
  357.8 5.8 %copy-start = (bf16[192,2048]{1,0:T(8,128)(2,1)S(1)}, bf16[192,2048]{1,0:T(8,128)(2,1)}, u32[]{:S(2)}) copy-start(bf16[192,2048]{1,0:T(8,128)(2,1)} %get-tuple-element.89) | copy-start | bytes 2359300
  357.8 6.7 %copy-start.3 = (f32[96,192]{1,0:T(8,128)S(1)}, f32[96,192]{1,0:T(8,128)}, u32[]{:S(2)}) copy-start(f32[96,192]{1,0:T(8,128)} %get-tuple-element.93) | copy-start | bytes 221188
